TPU v7x, 32 devices: a whole 2x2x4 slice. The times are simulated.
32 devices in a mesh: row: 8 (over z, x), col: 4 (over y, core).
Axes of the slice: x: 2, y: 2, z: 4, core: 2. Of those that a mesh axis runs over, the one named last changes fastest.
Arguments:
- panels: int32 [1], replicated, may hold values from 0 to 15
- inverse: float32 [16384, 16384], P('row', 'col'), may hold values from -4 to 28, as said below
- weight: float32 [1024, 16384], P('row', 'col'), may hold values from -0.046875 to 0.046875
- tokens: bfloat16 [1024, 16384], P('row', 'col'), may hold values from -6 to 6
- targets: bfloat16 [1024, 1024], P('row', 'col'), may hold values from -6 to 6
Outputs:
- new_inverse: float32 [16384, 16384], P('row', 'col')
- pruned: float32 [1024, 16384], P('row', 'col')
- residual: float32 [1024, 1024], P('row', 'col')
- correlation: float32 [1024, 16384], P('row', 'col')
Inputs may be any that keep to these rules, and one draw needn't show every extreme that they name: `inverse`: symmetric and positive definite.
All inputs are finite; a program needn't handle non-finite values.
Results may differ from a plain program's by a relative error of at most 0.0035.
Values may be sent and summed in bfloat16 or wider, within the bound.
No kernel may reach another device: no remote copies, remote signals or barrier semaphores. Data moves between devices by JAX's collectives and lax.ppermute only.
A program may use at most 192 MiB of HBM per device.

v0:
```python
import math

import jax
import jax.numpy as jnp
from jax import lax
from jax.sharding import PartitionSpec as P

PW = 1024


def broadcast(array, axis, root):
    mine = lax.axis_index(axis) == root
    return lax.psum(jnp.where(mine, array, jnp.zeros_like(array)), axis)


def cholesky_apply(factor, right_side):
    halfway = lax.linalg.triangular_solve(
        factor, right_side, left_side=True, lower=True, transpose_a=False
    )
    return lax.linalg.triangular_solve(
        factor, halfway, left_side=True, lower=True, transpose_a=True
    )


def shards(panels, inverse, weight, tokens, targets):
    highest = lax.Precision.HIGHEST
    rows_local = inverse.shape[0]
    cols_local = inverse.shape[1]
    out_local = targets.shape[1]
    anchor = panels[0] * PW
    owner_col = anchor // cols_local
    col_offset = anchor % cols_local
    owner_row = anchor // rows_local
    row_offset = anchor % rows_local
    holds_panel = lax.axis_index("col") == owner_col
    col_slab = lax.dynamic_slice_in_dim(inverse, col_offset, PW, 1)
    weight_slab = lax.dynamic_slice_in_dim(weight, col_offset, PW, 1)
    col_slab = jnp.where(holds_panel, col_slab, jnp.zeros_like(col_slab))
    weight_slab = jnp.where(holds_panel, weight_slab, jnp.zeros_like(weight_slab))
    col_share, weight_share = (
        lax.psum_scatter(col_slab, "col", scatter_dimension=0, tiled=True),
        lax.psum_scatter(weight_slab, "col", scatter_dimension=0, tiled=True),
    )
    col_slab, weight_slab = (
        lax.all_gather(col_share, "col", axis=0, tiled=True),
        lax.all_gather(weight_share, "col", axis=0, tiled=True),
    )
    row_slab = lax.dynamic_slice_in_dim(inverse, row_offset, PW, 0)
    diag_block = lax.dynamic_slice_in_dim(col_slab, row_offset, PW, 0)
    is_owner = lax.axis_index("row") == owner_row
    safe_block = jnp.where(is_owner, diag_block, jnp.eye(PW, dtype=jnp.float32))
    factor = jnp.linalg.cholesky(safe_block)
    solved = cholesky_apply(factor, row_slab)
    solved = broadcast(solved, "row", owner_row)
    new_inverse = inverse - jnp.dot(
        col_slab, solved, precision=highest, preferred_element_type=jnp.float32
    )
    pruned = weight - jnp.dot(
        weight_slab, solved, precision=highest, preferred_element_type=jnp.float32
    )
    pruned_low = pruned.astype(jnp.bfloat16)
    partial_value = lax.dot_general(
        tokens,
        lax.all_gather(pruned_low, "row", axis=0, tiled=True),
        (((1,), (1,)), ((), ())),
        preferred_element_type=jnp.float32,
    )
    col_index = lax.axis_index("col")
    placed = lax.dynamic_update_slice_in_dim(
        jnp.zeros_like(partial_value), targets.astype(jnp.float32), col_index * out_local, 1
    )
    partial_value = partial_value - placed
    residual = lax.psum_scatter(partial_value, "col", scatter_dimension=1, tiled=True)
    residual_low = lax.all_gather(residual.astype(jnp.bfloat16), "col", axis=1, tiled=True)
    token_count = tokens.shape[0] * lax.axis_size("row")
    correlation = lax.psum_scatter(
        lax.dot_general(
            residual_low, tokens, (((0,), (0,)), ((), ())), preferred_element_type=jnp.float32
        ),
        "row",
        scatter_dimension=0,
        tiled=True,
    )
    correlation = correlation * (1.0 / math.sqrt(token_count))
    return (new_inverse, pruned, residual, correlation)


def solution(mesh):
    in_specs = (P(), P("row", "col"), P("row", "col"), P("row", "col"), P("row", "col"))
    out_specs = (P("row", "col"), P("row", "col"), P("row", "col"), P("row", "col"))
    return jax.shard_map(shards, mesh=mesh, in_specs=in_specs, out_specs=out_specs, check_vma=False)
```

profile of v0, /device:TPU:0, one launch (start us, length us, event | category | flops | bytes accessed | tf_op | source)
XLA Modules:
  0.0 1669.7 jit_solution(16551720502229858485)
XLA Ops:
  8.0 9.3 constant_dynamic-slice_fusion.2
  17.3 9.1 copy.22
  26.4 5.0 broadcast_select_fusion.1
  31.5 77.9 %reduce-scatter.7.cloned.1.call-done = f32[512,1024]{0,1:T(8,128)} async-done(((f32[2048,1024]{0,1:T(8,128)}), f32[512,1024]{0,1:T(8,128)}) %reduce-scatter.7.cloned.1.call-update) | async-done | bytes 2097168 | tf_op jit(solution)/shard_map/reduce_scatter | solution.py:41
  112.2 57.2 %all-gather.3.cloned.1.call-done = f32[2048,1024]{0,1:T(8,128)} async-done(((f32[512,1024]{0,1:T(8,128)}), f32[2048,1024]{0,1:T(8,128)}) %all-gather.3.cloned.1.call-update) | async-done | bytes 8388624 | tf_op jit(solution)/shard_map/all_gather | solution.py:45
  169.4 5.5 convert_select_fusion
  174.9 5.5 copy.15
  180.4 4.8 fusion.46
  187.2 11.7 cholesky.223
  201.5 9.8 custom-call.64
  215.2 11.9 cholesky.244
  227.7 9.8 custom-call.65
  240.8 11.7 cholesky.468
  253.8 9.8 custom-call.66
  267.1 12.1 cholesky.487
  280.5 9.8 custom-call.67
  293.8 11.7 cholesky.506
  306.8 9.9 custom-call.68
  320.1 11.7 cholesky.526
  333.1 9.8 custom-call.69
  345.9 11.9 cholesky.546
  359.1 9.8 custom-call.70
  371.5 11.7 cholesky.564
  390.2 4.8 select_select_fusion
  395.0 23.2 %while.1 = (s32[]{:T(128)}, f32[1024,1024]{1,0:T(8,128)}, s32[8,2]{0,1:T(2,128)S(1)}, f32[8,128,128]{2,1,0:T(8,128)S(1)}, s32[]{:T(128)}) while((s32[]{:T(128)}, f32[1024,1024]{1,0:T(8,128)}, s32[8,2]{0,1:T(2,128)S(1)}, f32[8,128,128]{2,1,0:T(8,128)S(1)}, s32[]{:T(128)}) %tuple.63), condition=%wide.while_cond, body=%wide.while_body.sunk | while | flops 2 | bytes 131181 | solution.py:20
  418.2 79.0 %custom-call.71 = f32[8,128,128]{1,2,0:T(8,128)S(1)} custom-call(f32[8,128,128]{2,1,0:T(8,128)S(1)} %get-tuple-element.11), custom_call_target="InvertDiagBlocksLowerTriangular" | custom-call | tf_op jit(solution)/shard_map/triangular_solve | solution.py:20
  497.2 6.0 constant_dynamic-update-slice_fusion.10
  506.9 4.2 constant_dynamic-update-slice_fusion.9
  519.4 5.7 fusion.31
  529.3 7.4 fusion.37
  541.0 7.7 convolution_subtract_fusion.6
  552.7 10.6 convolution_subtract_fusion.5
  566.6 12.0 convolution_subtract_fusion.10
  596.6 4.4 fusion.34
  610.7 8.7 convolution_subtract_fusion.2
  630.2 9.8 convolution_subtract_fusion.1
  652.3 11.5 convolution_subtract_fusion.9
  677.6 6.4 broadcast_select_fusion
  684.0 8.2 all_gather.13
  692.2 504.8 %all-reduce.3.cloned.1.call-done = f32[1024,4096]{1,0:T(8,128)} async-done(((f32[1024,4096]{1,0:T(8,128)}), f32[1024,4096]{1,0:T(8,128)}) %all-reduce.3.cloned.1.call-update) | async-done | bytes 16777232 | tf_op jit(solution)/shard_map/psum | solution.py:13
  1197.0 13.9 fusion.113
  1211.2 123.9 %all-gather.5.cloned.1.call-done = bf16[1024,4096]{1,0:T(8,128)(2,1)} async-done(((bf16[128,4096]{1,0:T(8,128)(2,1)}), bf16[1024,4096]{1,0:T(8,128)(2,1)}) %all-gather.5.cloned.1.call-update) | async-done | bytes 8388624 | tf_op jit(solution)/shard_map/all_gather | solution.py:64
  1335.1 6.5 fusion.49
  1341.6 19.9 %reduce-scatter.9.cloned.1.call-done = f32[128,256]{0,1:T(8,128)} async-done(((f32[128,1024]{0,1:T(8,128)}), f32[128,256]{0,1:T(8,128)}) %reduce-scatter.9.cloned.1.call-update) | async-done | bytes 131088 | tf_op jit(solution)/shard_map/reduce_scatter | solution.py:73
  1362.5 5.8 all_gather.15
  1368.3 8.0 fusion.114
  1376.3 114.6 %convolution_subtract_fusion = f32[2048,4096]{1,0:T(8,128)} fusion(f32[2048,4096]{1,0:T(8,128)} %param.6, f32[2048,1024]{0,1:T(8,128)} %all-gather.3.cloned.1.call-done, f32[1024,4096]{1,0:T(8,128)} %all-reduce.3.cloned.1.call-done), kind=kOutput, calls=%fused_computation.2 | convolution fusion | flops 103087603712 | bytes 92274688 | tf_op jit(solution)/shard_map/dot_general | solution.py:55
  1491.7 167.6 %reduce-scatter.11.cloned.1.call-done = f32[128,4096]{1,0:T(8,128)} async-done(((f32[1024,4096]{1,0:T(8,128)}), f32[128,4096]{1,0:T(8,128)}) %reduce-scatter.11.cloned.1.call-update) | async-done | bytes 2097168 | tf_op jit(solution)/shard_map/reduce_scatter | solution.py:76
  (146 shorter events, 159.8 us)
Async XLA Ops:
  7.2 1327.9 %copy-start = (bf16[128,4096]{1,0:T(8,128)(2,1)S(1)}, bf16[128,4096]{1,0:T(8,128)(2,1)}, u32[]{:S(2)}) copy-start(bf16[128,4096]{1,0:T(8,128)(2,1)} %param.8) | copy-start | bytes 3145732
  7.2 102.3 %reduce-scatter.7.cloned.1.call-start = ((), (), s32[]{:S(2)}) async-start(), calls=%async_computation.4 | async-start | bytes 10485760 | tf_op jit(solution)/shard_map/reduce_scatter | solution.py:41
  31.5 137.9 %all-gather.3.cloned.1.call-start = ((), (), s32[]{:S(2)}) async-start(), calls=%async_computation.5 | async-start | bytes 10485760 | tf_op jit(solution)/shard_map/all_gather | solution.py:45
  109.5 574.6 %reduce-scatter.13.cloned.1.call-start = ((), (), s32[]{:S(2)}) async-start(), calls=%async_computation.10 | async-start | bytes 655360 | tf_op jit(solution)/shard_map/reduce_scatter | solution.py:42
  112.0 1085.0 %all-reduce.3.cloned.1.call-start = ((), (), s32[]{:S(2)}) async-start(), calls=%async_computation.6 | async-start | bytes 33554432 | tf_op jit(solution)/shard_map/psum | solution.py:13
  185.2 1.9 copy-start.2
  497.2 6.0 copy-start.1
  529.3 7.4 copy-start.4
  594.7 1.9 copy-start.5
  683.9 513.1 %copy-start.3 = (f32[128,4096]{1,0:T(8,128)S(1)}, f32[128,4096]{1,0:T(8,128)}, u32[]{:S(2)}) copy-start(f32[128,4096]{1,0:T(8,128)} %param.7) | copy-start | bytes 6291460
  684.0 651.1 %all-gather.5.cloned.1.call-start = ((), (), s32[]{:S(2)}) async-start(), calls=%async_computation.7 | async-start | bytes 9437184 | tf_op jit(solution)/shard_map/all_gather | solution.py:64
  692.2 518.8 %copy-start.7 = (bf16[128,256]{1,0:T(8,128)(2,1)S(1)}, bf16[128,256]{1,0:T(8,128)(2,1)}, u32[]{:S(2)}) copy-start(bf16[128,256]{1,0:T(8,128)(2,1)} %param.9) | copy-start | bytes 196612
  1210.9 150.7 %reduce-scatter.9.cloned.1.call-start = ((), (), s32[]{:S(2)}) async-start(), calls=%async_computation.8 | async-start | bytes 655360 | tf_op jit(solution)/shard_map/reduce_scatter | solution.py:73
  1341.6 317.7 %reduce-scatter.11.cloned.1.call-start = ((), (), s32[]{:S(2)}) async-start(), calls=%async_computation.9 | async-start | bytes 18874368 | tf_op jit(solution)/shard_map/reduce_scatter | solution.py:76
  1376.3 114.6 %copy-start.6 = (f32[128,256]{0,1:T(8,128)S(1)}, f32[128,256]{0,1:T(8,128)}, u32[]{:S(2)}) copy-start(f32[128,256]{0,1:T(8,128)} %reduce-scatter.9.cloned.1.call-done) | copy-start | bytes 393220
Sparse Core Ops, SparseCore 0:
  31.6 77.7 reduce-scatter.6
  111.1 58.2 all-gather.2
  172.6 21.7 reduce-scatter.12
  684.1 512.8 all-reduce.2
  1211.0 123.9 all-gather.4
  1341.7 19.8 reduce-scatter.8
  1376.4 282.7 reduce-scatter.10
where the time goes:
time: 1680 us; the launch traced here: 1670 us
  waiting for transfers between devices  951 us (57%)
  matrix products  312 us (19%)
  other arithmetic  282 us (17%)
  local copies, waits for them, and re-layouts  88.6 us (5%)
  between operations  20.8 us (1%)
    psum x1, waiting for transfers between devices, broadcast(): return lax.psum(jnp.where(mine, array, jnp.zeros_like(array)), axis)  505 us
    another operation x30, other arithmetic, shards(): factor = jnp.linalg.cholesky(safe_block)  172 us
    reduce_scatter x1, waiting for transfers between devices, shards(): lax.psum_scatter(lax.dot_general(residual_low, tokens, (((0,), (0,)), (()...  168 us
    all_gather x1, waiting for transfers between devices, shards(): lax.all_gather(pruned_low, 'row', axis=0, tiled=True)  124 us
    dot_general x1, matrix products, shards(): jnp.dot(col_slab, solved, precision=highest, preferred_element_type=jnp.f...  115 us
    another operation x3, other arithmetic, cholesky_apply(): lax.linalg.triangular_solve(factor, halfway, left_side=True, lower=True,...  83.8 us
    another operation x15, matrix products, cholesky_apply(): lax.linalg.triangular_solve(factor, right_side, left_side=True, lower=Tru...  83.2 us
    reduce_scatter x1, waiting for transfers between devices, shards(): lax.psum_scatter(col_slab, 'col', scatter_dimension=0, tiled=True)  77.9 us
  transfers between devices with their start and end apart: 7, of which 6 were waited for; matrix products, arithmetic and copies ran while one was open for 37% of the time, Pallas kernels for 0%

commit v1 on v0

v1 whole, which is shorter than its diff:
```python
import functools
import math

import jax
import jax.numpy as jnp
from jax import lax
from jax.experimental import pallas as pl
from jax.experimental.pallas import tpu as pltpu
from jax.sharding import PartitionSpec as P

PW = 1024
TILE = 256
NB = 128
CHUNKS = 4

BF16 = jnp.bfloat16
F32 = jnp.float32


def bits(n):
    return [1 << b for b in range(n.bit_length() - 1)]


def swap(x, axis, bit):
    n = lax.axis_size(axis)
    return lax.ppermute(x, axis, [(i, i ^ bit) for i in range(n)])


def joint(pairs, cols):
    return [(a * cols + c, b * cols + d) for (a, c), (b, d) in pairs]


def pick(cond, a, b):
    return jnp.where(cond, a, b), jnp.where(cond, b, a)


def scatter_step(x, bit, root):
    col = lax.axis_index("col")
    low = (col & bit) == 0
    mine, other = pick(low, x[0::2], x[1::2])
    got = swap(other, "col", bit)
    return jnp.where(((col ^ root) & bit) == 0, mine, got)


def gather_step(x, bit):
    low = (lax.axis_index("col") & bit) == 0
    got = swap(x, "col", bit)
    a, b = pick(low, x, got)
    return jnp.stack([a, b], 1).reshape((2 * x.shape[0],) + x.shape[1:])


def spread_step(x, axis, bit, root):
    got = swap(x, axis, bit)
    return jnp.where(((lax.axis_index(axis) ^ root) & bit) == 0, x, got)


def spread_block(block, owner_row, owner_col):
    n_row, n_col = lax.axis_size("row"), lax.axis_size("col")
    for bit in bits(n_col):
        block = scatter_step(block, bit, owner_col)
    for bit in bits(n_row):
        block = spread_step(block, "row", bit, owner_row)
    for bit in reversed(bits(n_col)):
        block = gather_step(block, bit)
    return block


def spread_col(x, owner_col):
    steps = bits(lax.axis_size("col"))
    x = spread_step(x, "col", steps[0], owner_col)
    half = x.shape[0] // 2
    side = lax.axis_index("col") & 1
    part = lax.dynamic_slice_in_dim(x, side * half, half, 0)
    for bit in steps[1:]:
        part = spread_step(part, "col", bit, owner_col)
    got = swap(part, "col", 1)
    a, b = pick(side == 0, part, got)
    return jnp.concatenate([a, b], 0)


def spread_row(x):
    n_row, n_col = lax.axis_size("row"), lax.axis_size("col")
    k = n_row // n_col
    row, col = lax.axis_index("row"), lax.axis_index("col")
    open_bits = n_col - 1
    for bit in reversed(bits(n_col)):
        pairs = [
            ((hi * k + lo, c), ((hi ^ bit) * k + lo, c))
            for c in range(n_col)
            for hi in range(n_col)
            for lo in range(k)
            if (hi ^ c) & open_bits == 0
        ]
        open_bits &= ~bit
        got = lax.ppermute(x, ("row", "col"), joint(pairs, n_col))
        x = jnp.where((((row // k) ^ col) & bit) == 0, x, got)
    x = x[None]
    for bit in reversed(bits(k)):
        got = swap(x, "row", bit)
        a, b = pick((row & bit) == 0, x, got)
        x = jnp.stack([a, b], 1).reshape((2 * x.shape[0],) + x.shape[1:])
    return x


def gather_rows(x):
    x = x[None]
    order = [0]
    for bit in reversed(bits(lax.axis_size("row"))):
        got = swap(x, "row", bit)
        x = jnp.concatenate([x, got], 0)
        order = order + [o ^ bit for o in order]
    return x, order


def dot32(a, b):
    ah, bh = a.astype(BF16), b.astype(BF16)
    al, bl = (a - ah.astype(F32)).astype(BF16), (b - bh.astype(F32)).astype(BF16)
    dot = functools.partial(jnp.dot, preferred_element_type=F32)
    return dot(ah, bh) + (dot(ah, bl) + dot(al, bh))


def wide(x, n):
    return jnp.broadcast_to(x, (x.shape[0], n))


def sweep_panel(t, k, lane, sub):
    n = t.shape[1]
    for j in range(0, 8, 2):
        c0, c1 = wide(t[:, k + j : k + j + 1], n), wide(t[:, k + j + 1 : k + j + 2], n)
        r0, r1 = t[j : j + 1, :], t[j + 1 : j + 2, :]
        p, q = c0[j : j + 1, :], c1[j : j + 1, :]
        q2, s = c0[j + 1 : j + 2, :], c1[j + 1 : j + 2, :]
        inv = 1.0 / (p * s - q * q2)
        on0, on1 = lane == k + j, lane == k + j + 1
        b0 = jnp.where(on0, 1.0, jnp.where(on1, 0.0, r0))
        b1 = jnp.where(on0, 0.0, jnp.where(on1, 1.0, r1))
        e0 = (s * b0 - q * b1) * inv
        e1 = (p * b1 - q2 * b0) * inv
        a0 = jnp.where(on0, e0 + 1.0, e0)
        a1 = jnp.where(on1, e1 + 1.0, e1)
        u = t - c0 * a0 - c1 * a1
        t = jnp.where(sub == j, e0, jnp.where(sub == j + 1, e1, u))
    return t


def sweep(t):
    n = t[0].shape[1]
    lane = lax.broadcasted_iota(jnp.int32, (1, n), 1)
    sub = lax.broadcasted_iota(jnp.int32, (8, n), 0)
    t = list(t)
    count = len(t)
    for at in range(count):
        k = 8 * at
        new = sweep_panel(t[at], k, lane, sub)
        inside = (lane >= k) & (lane < k + 8)
        rows = [jnp.broadcast_to(new[j : j + 1, :], (8, n)) for j in range(8)]
        for i in [(at + 1 + step) % count for step in range(count - 1)]:
            u = jnp.where(inside, 0.0, t[i])
            for j in range(8):
                u = u - wide(t[i][:, k + j : k + j + 1], n) * rows[j]
            t[i] = u
        t[at] = new
    return t


def inverse_kernel(packed_ref, high_ref, low_ref, a_ref):
    n = a_ref.shape[0]
    at = 0
    for i in range(n // TILE):
        for j in range(i + 1):
            part = packed_ref[at * TILE : (at + 1) * TILE, :]
            a_ref[i * TILE : (i + 1) * TILE, j * TILE : (j + 1) * TILE] = part
            if i != j:
                a_ref[j * TILE : (j + 1) * TILE, i * TILE : (i + 1) * TILE] = part.T
            at += 1
    eye = (
        lax.broadcasted_iota(jnp.int32, (NB, NB), 0) == lax.broadcasted_iota(jnp.int32, (NB, NB), 1)
    ).astype(F32)

    def step(k, _):
        o = pl.multiple_of(k * NB, NB)
        t = [
            a_ref[pl.ds(pl.multiple_of(o + 8 * i, 8), 8), pl.ds(o, NB)] for i in range(NB // 8)
        ]
        pivot = jnp.concatenate(sweep(t), 0)
        a_ref[pl.ds(o, NB), pl.ds(o, NB)] = eye
        new = dot32(pivot, a_ref[pl.ds(o, NB), :])

        def update(i, _):
            r = pl.multiple_of(i * TILE, TILE)
            c = a_ref[pl.ds(r, TILE), pl.ds(o, NB)]
            a_ref[pl.ds(r, TILE), pl.ds(o, NB)] = jnp.zeros((TILE, NB), F32)
            a_ref[pl.ds(r, TILE), :] = a_ref[pl.ds(r, TILE), :] - dot32(c, new)
            return 0

        lax.fori_loop(0, n // TILE, update, 0)
        a_ref[pl.ds(o, NB), :] = new
        return 0

    lax.fori_loop(0, n // NB, step, 0)

    def store(i, _):
        r = pl.multiple_of(i * NB, NB)
        a = a_ref[pl.ds(r, NB), :]
        high = a.astype(BF16)
        high_ref[pl.ds(r, NB), :] = high
        low_ref[pl.ds(r, NB), :] = (a - high.astype(F32)).astype(BF16)
        return 0

    lax.fori_loop(0, n // NB, store, 0)


def block_inverse(packed):
    shape = jax.ShapeDtypeStruct((PW, PW), BF16)
    return pl.pallas_call(
        inverse_kernel,
        out_shape=(shape, shape),
        in_specs=[pl.BlockSpec(memory_space=pltpu.VMEM)],
        out_specs=(pl.BlockSpec(memory_space=pltpu.VMEM),) * 2,
        scratch_shapes=[pltpu.VMEM((PW, PW), F32)],
        compiler_params=pltpu.CompilerParams(vmem_limit_bytes=32 << 20),
        cost_estimate=pl.CostEstimate(flops=60 * PW**3, bytes_accessed=8 * PW**2, transcendentals=0),
    )(packed)


def pack(block):
    parts = [
        block[i * TILE : (i + 1) * TILE, j * TILE : (j + 1) * TILE]
        for i in range(PW // TILE)
        for j in range(i + 1)
    ]
    return jnp.concatenate(parts, 0)


def nt(a, b):
    return lax.dot_general(a, b, (((1,), (1,)), ((), ())), preferred_element_type=F32)


def nn(a, b):
    return lax.dot_general(a, b, (((1,), (0,)), ((), ())), preferred_element_type=F32)


def shards(panels, inverse, weight, tokens, targets):
    n_row, n_col = lax.axis_size("row"), lax.axis_size("col")
    k = n_row // n_col
    row, col = lax.axis_index("row"), lax.axis_index("col")
    rows_local, cols_local = inverse.shape
    out_rows = weight.shape[0]
    token_rows = tokens.shape[0]
    anchor = panels[0] * PW
    owner_col, col_offset = anchor // cols_local, anchor % cols_local
    owner_row, row_offset = anchor // rows_local, anchor % rows_local

    block = pack(lax.dynamic_slice(inverse, (row_offset, col_offset), (PW, PW)))
    block = spread_block(block.reshape(n_col, -1, TILE), owner_row, owner_col).reshape(-1, TILE)
    high, low = block_inverse(block)

    weight_slab = lax.dynamic_slice_in_dim(weight, col_offset, PW, 1).astype(BF16)
    weight_slab = spread_col(weight_slab, owner_col)
    size = rows_local // CHUNKS
    own, across = [], []
    for i in range(CHUNKS):
        part = lax.dynamic_slice(inverse, (i * size, col_offset), (size, PW)).astype(BF16)
        part = spread_col(part, owner_col)
        own.append(part)
        across.append(spread_row(part))
    column = jnp.concatenate(own, 0)
    panel = jnp.stack(across, 1).reshape(cols_local, PW)

    all_tokens, order = gather_rows(tokens)
    all_tokens = all_tokens.reshape(-1, tokens.shape[1])

    held = []
    for i in order:
        pairs = [
            ((r, (r ^ i) // k), (r ^ i, (r ^ i) // k)) for r in range(n_row)
        ]
        tile = lax.dynamic_slice_in_dim(targets, ((row ^ i) % k) * out_rows, out_rows, 1)
        held.append(lax.ppermute(tile, ("row", "col"), joint(pairs, n_col)))
    held = jnp.concatenate(held, 0).astype(F32)

    mixed = nn(jnp.concatenate([column, column], 1), jnp.concatenate([high, low], 0))
    place = lax.broadcasted_iota(jnp.int32, mixed.shape, 0) - row_offset
    unit = (place == lax.broadcasted_iota(jnp.int32, mixed.shape, 1)).astype(F32)
    inside = (row == owner_row) & (place >= 0) & (place < PW)
    mixed = jnp.where(inside, unit, mixed).astype(BF16)

    mixed_weight = nn(
        jnp.concatenate([weight_slab, weight_slab], 1), jnp.concatenate([high, low], 0)
    ).astype(BF16)
    pruned = weight - nt(mixed_weight, panel)
    pruned_low = pruned.astype(BF16)

    value = nt(all_tokens, pruned_low) - held
    for bit in bits(n_col):
        value = value + swap(value, "col", bit)
    new_inverse = inverse - nt(mixed, panel)
    value_low = value.astype(BF16)
    correlation = lax.dot_general(
        value_low, all_tokens, (((0,), (0,)), ((), ())), preferred_element_type=F32
    ) * (1.0 / math.sqrt(token_rows * n_row))

    tiles = [jnp.zeros((token_rows, out_rows), F32)] * k
    for at, i in enumerate(order):
        pairs = [((r, r // k), (r ^ i, r // k)) for r in range(n_row)]
        tile = lax.ppermute(
            value[at * token_rows : (at + 1) * token_rows], ("row", "col"), joint(pairs, n_col)
        )
        for lo in range(k):
            tiles[lo] = tiles[lo] + jnp.where((row ^ i) % k == lo, tile, 0.0)
    residual = jnp.concatenate(tiles, 1)
    return (new_inverse, pruned, residual, correlation)


def solution(mesh):
    in_specs = (P(), P("row", "col"), P("row", "col"), P("row", "col"), P("row", "col"))
    out_specs = (P("row", "col"), P("row", "col"), P("row", "col"), P("row", "col"))
    return jax.shard_map(shards, mesh=mesh, in_specs=in_specs, out_specs=out_specs, check_vma=False)
```

time: 1680 us -> 585 us (0.35)
  waiting for transfers between devices: 951 us -> 230 us
  other arithmetic: 282 us -> 21.4 us
  matrix products: 312 us -> 65.3 us
  starting transfers between devices: 0.29 us -> 158 us
  Pallas kernels: 0 us -> 75.2 us
  local copies, waits for them, and re-layouts: 88.6 us -> 23.6 us
  between operations: 20.8 us -> 2.75 us
    psum x1 -> x0, waiting for transfers between devices: 505 us -> none  [broadcast(): return lax.psum(jnp.where(mine, array, jnp.zeros_like(array)), axis)]
    reduce_scatter x4 -> x0, waiting for transfers between devices: 265 us -> none  [the longest x1 168 us: shards(): lax.psum_scatter(lax.dot_general(residual_low, tokens, (((0,), (0,)), (()...]
    another operation x33 -> x10, other arithmetic: 256 us -> 5.68 us  [the longest x3 4.59 us: shards(): panel = jnp.stack(across, 1).reshape(cols_local, PW)]
    ppermute x0 -> x55, waiting for transfers between devices: none -> 230 us  [the longest x31 206 us: swap(): return lax.ppermute(x, axis, [(i, i ^ bit) for i in range(n)])]
    all_gather x2 -> x0, waiting for transfers between devices: 181 us -> none  [the longest x1 124 us: shards(): lax.all_gather(pruned_low, 'row', axis=0, tiled=True)]
    another operation x44 -> x0, matrix products: 169 us -> none  [the longest x15 83.2 us: cholesky_apply(): lax.linalg.triangular_solve(factor, right_side, left_side=True, lower=Tru...]
    ppermute x0 -> x55, starting transfers between devices: none -> 158 us  [the longest x31 112 us: swap(): return lax.ppermute(x, axis, [(i, i ^ bit) for i in range(n)])]
    dot_general x4 -> x5, matrix products: 143 us -> 65.3 us  [the longest x3 45.2 us: nt(): lax.dot_general(a, b, (((1,), (1,)), ((), ())), preferred_element_type=F32)]
  transfers between devices with their start and end apart: 7 -> 55, of which waited for: 6 -> 16; matrix products, arithmetic and copies ran while one was open for 37% -> 17% of each run, Pallas kernels for 0% -> 13%
where the time goes in v1:
time: 585 us; the launch traced here: 576 us
  waiting for transfers between devices  230 us (39%)
  starting transfers between devices  158 us (27%)
  Pallas kernels  75.2 us (13%)
  matrix products  65.3 us (11%)
  local copies, waits for them, and re-layouts  23.6 us (4%)
  other arithmetic  21.4 us (4%)
    ppermute x31, waiting for transfers between devices, swap(): return lax.ppermute(x, axis, [(i, i ^ bit) for i in range(n)])  206 us
    ppermute x31, starting transfers between devices, swap(): return lax.ppermute(x, axis, [(i, i ^ bit) for i in range(n)])  112 us
    pallas_call x1, Pallas kernels, block_inverse(): pl.pallas_call(inverse_kernel, out_shape=(shape, shape), in_specs=[pl.Blo...  75.2 us
    dot_general x3, matrix products, nt(): lax.dot_general(a, b, (((1,), (1,)), ((), ())), preferred_element_type=F32)  45.2 us
    ppermute x8, waiting for transfers between devices, shards(): held.append(lax.ppermute(tile, ('row', 'col'), joint(pairs, n_col)))  23.1 us
    ppermute x8, starting transfers between devices, spread_row(): got = lax.ppermute(x, ('row', 'col'), joint(pairs, n_col))  19.1 us
    ppermute x8, starting transfers between devices, shards(): lax.ppermute(value[at * token_rows:(at + 1) * token_rows], ('row', 'col')...  15.8 us
    dot_general x1, matrix products, nn(): lax.dot_general(a, b, (((1,), (0,)), ((), ())), preferred_element_type=F32)  14.1 us
  transfers between devices with their start and end apart: 55, of which 16 were waited for; matrix products, arithmetic and copies ran while one was open for 17% of the time, Pallas kernels for 13%

profile of v1, /device:TPU:0, one launch (start us, length us, event | category | flops | bytes accessed | tf_op | source)
XLA Modules:
  0.0 576.2 jit_solution(14995750639844332494)
XLA Ops:
  8.3 1.4 dynamic-slice_dynamic-update-slice_fusion
  9.7 7.3 %dynamic-slice_convert_fusion = (bf16[512,1024]{1,0:T(8,128)(2,1)}, bf16[512,1024]{1,0:T(8,128)(2,1)}, bf16[512,1024]{1,0:T(8,128)(2,1)}, bf16[512,1024]{1,0:T(8,128)(2,1)}) fusion(f32[2048,4096]{1,0:T(8,128)} %param.6, s32[]{:T(128)S(6)} %select_n.487), kind=kLoop, calls=%fused_computation.20 | loop fusion | bytes 8388612 | tf_op jit(solution)/shard_map/convert_element_type | solution.py:263
  28.8 2.6 collective-permute-start.31
  31.4 2.8 collective-permute-start.34
  34.2 3.1 collective-permute-start.41
  38.7 20.1 %collective-permute-done.40 = bf16[128,128]{1,0:T(8,128)(2,1)S(1)} collective-permute-done((bf16[128,128]{1,0:T(8,128)(2,1)S(1)}, bf16[128,128]{1,0:T(8,128)(2,1)S(1)}, u32[]{:S(2)}, u32[]{:S(2)}) %collective-permute-start.40) | collective-permute-done | bytes 32800 | tf_op jit(solution)/shard_map/ppermute | solution.py:279
  60.1 3.6 collective-permute-done.32
  63.8 20.1 %collective-permute-start.9 = (bf16[512,1024]{1,0:T(8,128)(2,1)}, bf16[512,1024]{1,0:T(8,128)(2,1)S(1)}, u32[]{:S(2)}, u32[]{:S(2)}) collective-permute-start(bf16[512,1024]{1,0:T(8,128)(2,1)} %get-tuple-element.24), channel_id=1, source_target_pairs={{0,1},{1,0},{2,3},{3,2},{4,5},{5,4},{6,7},{7,6},{8,9},{9,8},{10,11... | collective-permute-start | bytes 3145736 | tf_op jit(solution)/shard_map/ppermute | solution.py:26
  84.0 3.0 collective-permute-done.43
  88.2 1.5 pad_maximum_fusion.4
  89.8 2.3 collective-permute-start.35
  97.6 9.5 %collective-permute-done.10 = bf16[256,1024]{1,0:T(8,128)(2,1)S(1)} collective-permute-done((bf16[256,1024]{1,0:T(8,128)(2,1)S(1)}, bf16[256,1024]{1,0:T(8,128)(2,1)S(1)}, u32[]{:S(2)}, u32[]{:S(2)}) %collective-permute-start.10) | collective-permute-done | bytes 524320 | tf_op jit(solution)/shard_map/ppermute | solution.py:26
  108.0 10.4 %collective-permute-done.7 = bf16[256,1024]{1,0:T(8,128)(2,1)S(1)} collective-permute-done((bf16[256,1024]{1,0:T(8,128)(2,1)S(1)}, bf16[256,1024]{1,0:T(8,128)(2,1)S(1)}, u32[]{:S(2)}, u32[]{:S(2)}) %collective-permute-start.7) | collective-permute-done | bytes 524320 | tf_op jit(solution)/shard_map/ppermute | solution.py:26
  118.5 22.4 %collective-permute-done.1 = bf16[256,1024]{1,0:T(8,128)(2,1)S(1)} collective-permute-done((bf16[256,1024]{1,0:T(8,128)(2,1)S(1)}, bf16[256,1024]{1,0:T(8,128)(2,1)S(1)}, u32[]{:S(2)}, u32[]{:S(2)}) %collective-permute-start.1) | collective-permute-done | bytes 524320 | tf_op jit(solution)/shard_map/ppermute | solution.py:26
  141.6 12.4 %collective-permute-done.13 = f32[1,640,256]{2,1,0:T(8,128)S(1)} collective-permute-done((f32[1,640,256]{2,1,0:T(8,128)S(1)}, f32[1,640,256]{2,1,0:T(8,128)S(1)}, u32[]{:S(2)}, u32[]{:S(2)}) %collective-permute-start.13) | collective-permute-done | bytes 655392 | tf_op jit(solution)/shard_map/ppermute | solution.py:26
  155.9 3.3 collective-permute-start.19
  159.7 1.4 collective-permute-start.22
  161.5 1.4 collective-permute-start.25
  163.4 8.0 %collective-permute-done.14 = f32[1,640,256]{2,1,0:T(8,128)S(1)} collective-permute-done((f32[1,640,256]{2,1,0:T(8,128)S(1)}, f32[1,640,256]{2,1,0:T(8,128)S(1)}, u32[]{:S(2)}, u32[]{:S(2)}) %collective-permute-start.14) | collective-permute-done | bytes 655392 | tf_op jit(solution)/shard_map/ppermute | solution.py:26
  171.3 3.0 collective-permute-start.28
  174.6 2.4 pad_maximum_fusion.2
  177.1 43.1 %collective-permute-start.36 = (bf16[4,128,4096]{2,1,0:T(8,128)(2,1)}, bf16[4,128,4096]{2,1,0:T(8,128)(2,1)}, u32[]{:S(2)}, u32[]{:S(2)}) collective-permute-start(bf16[4,128,4096]{2,1,0:T(8,128)(2,1)} %pad_maximum_fusion.2), channel_id=1, source_target_pairs={{0,4},{4,0},{8,12},{12,8},{16,20},{20,16},{24,28},{28,24},{1,5},{5... | collective-permute-start | bytes 12582920 | tf_op jit(solution)/shard_map/ppermute | solution.py:26
  220.7 4.2 collective-permute-start.20
  225.0 2.5 collective-permute-start.16
  228.0 1.4 collective-permute-start.23
  229.8 1.4 collective-permute-start.26
  231.6 23.0 %collective-permute-done.16 = f32[1,640,256]{2,1,0:T(8,128)S(1)} collective-permute-done((f32[1,640,256]{2,1,0:T(8,128)S(1)}, f32[1,640,256]{2,1,0:T(8,128)S(1)}, u32[]{:S(2)}, u32[]{:S(2)}) %collective-permute-start.16) | collective-permute-done | bytes 655392 | tf_op jit(solution)/shard_map/ppermute | solution.py:26
  254.5 3.2 collective-permute-start.29
  257.8 24.3 %collective-permute-start.17 = (f32[1,640,256]{2,1,0:T(8,128)S(1)}, f32[1,640,256]{2,1,0:T(8,128)S(1)}, u32[]{:S(2)}, u32[]{:S(2)}) collective-permute-start(f32[1,640,256]{2,1,0:T(8,128)S(1)} %broadcast_select_fusion.18), channel_id=1, source_target_pairs={{0,2},{1,3},{2,0},{3,1},{4,6},{5,7},{6,4},{7,5},{8,10},{9,11},{10,... | collective-permute-start | bytes 1966088 | tf_op jit(solution)/shard_map/ppermute | solution.py:26
  284.6 1.4 collective-permute-start.27
  286.2 4.5 collective-permute-done.17
  292.0 44.2 %collective-permute-done.21 = bf16[1,512,1024]{2,1,0:T(8,128)(2,1)S(1)} collective-permute-done((bf16[1,512,1024]{2,1,0:T(8,128)(2,1)S(1)}, bf16[1,512,1024]{2,1,0:T(8,128)(2,1)S(1)}, u32[]{:S(2)}, u32[]{:S(2)}) %collective-permute-start.21) | collective-permute-done | bytes 1048608 | tf_op jit(solution)/shard_map/ppermute | solution.py:26
  336.3 22.3 %collective-permute-done.24 = bf16[1,512,1024]{2,1,0:T(8,128)(2,1)S(1)} collective-permute-done((bf16[1,512,1024]{2,1,0:T(8,128)(2,1)S(1)}, bf16[1,512,1024]{2,1,0:T(8,128)(2,1)S(1)}, u32[]{:S(2)}, u32[]{:S(2)}) %collective-permute-start.24) | collective-permute-done | bytes 1048608 | tf_op jit(solution)/shard_map/ppermute | solution.py:26
  358.8 22.3 %collective-permute-done.27 = bf16[1,512,1024]{2,1,0:T(8,128)(2,1)S(1)} collective-permute-done((bf16[1,512,1024]{2,1,0:T(8,128)(2,1)S(1)}, bf16[1,512,1024]{2,1,0:T(8,128)(2,1)S(1)}, u32[]{:S(2)}, u32[]{:S(2)}) %collective-permute-start.27) | collective-permute-done | bytes 1048608 | tf_op jit(solution)/shard_map/ppermute | solution.py:26
  381.7 21.5 %collective-permute-done.30 = bf16[1,512,1024]{2,1,0:T(8,128)(2,1)S(1)} collective-permute-done((bf16[1,512,1024]{2,1,0:T(8,128)(2,1)S(1)}, bf16[1,512,1024]{2,1,0:T(8,128)(2,1)S(1)}, u32[]{:S(2)}, u32[]{:S(2)}) %collective-permute-start.30) | collective-permute-done | bytes 1048608 | tf_op jit(solution)/shard_map/ppermute | solution.py:26
  403.7 3.9 pad_maximum_fusion
  408.0 75.2 %shard_map.84 = (bf16[1024,1024]{1,0:T(8,128)(2,1)S(1)}, bf16[1024,1024]{1,0:T(8,128)(2,1)S(1)}) custom-call(f32[2560,256]{1,0:T(8,128)S(1)} %bitcast.71), custom_call_target="tpu_custom_call" | custom-call | flops 64424509440 | bytes 8388608 | tf_op jit(solution)/shard_map/pallas_call | solution.py:215
  483.6 2.0 copy-done.1
  485.6 10.0 %convolution_subtract_fusion.1 = f32[128,4096]{1,0:T(8,128)} fusion(f32[128,4096]{1,0:T(8,128)} %param.7, bf16[4096,1024]{1,0:T(8,128)(2,1)} %bitcast.74, bf16[2048,1024]{1,0:T(8,128)(2,1)} %copy-done.1, bf16[64,1024]{1,0:T(8,128)(2,1)S(1)} %get-tuple-element.49, bf16[64,1024]{1,0:T(8,128)(2,1)S(1)} %get-tuple-element.48), kind=kOutput, calls=%fused_computation.10 | convolution fusion | flops 1613365248 | bytes 17039360 | tf_op jit(solution)/shard_map/dot_general | solution.py:236
  495.7 3.9 pad_maximum_fusion.1
  499.6 2.3 convolution_subtract_fusion.2
  502.9 1.9 collective-permute-done.45
  504.8 1.5 collective-permute-start.46
  506.3 14.1 %select_convert_fusion.4 = bf16[2048,1024]{1,0:T(8,128)(2,1)} fusion(bf16[2048,1024]{1,0:T(8,128)(2,1)} %copy-done.1, bf16[2048,1024]{1,0:T(8,128)(2,1)} %copy-done.11, s32[2048]{0:T(1024)S(1)} %iota_subtract_fusion, pred[2048]{0:T(1024)(128)(4,1)S(1)} %compare_and_fusion), kind=kOutput, calls=%fused_computation.7.clone.clone.1 | convolution fusion | flops 8615100416 | bytes 12593152 | tf_op jit(solution)/shard_map/dot_general | solution.py:240
  521.2 5.3 collective-permute-start.54
  527.8 32.8 %convolution_subtract_fusion = f32[2048,4096]{1,0:T(8,128)} fusion(f32[2048,4096]{1,0:T(8,128)} %param.6, bf16[4096,1024]{1,0:T(8,128)(2,1)} %bitcast.75, bf16[2048,1024]{1,0:T(8,128)(2,1)} %select_convert_fusion.4), kind=kOutput, calls=%fused_computation | convolution fusion | flops 17188257792 | bytes 79691776 | tf_op jit(solution)/shard_map/dot_general | solution.py:236
  561.9 3.4 collective-permute-start.51
  569.2 6.0 %convolution_multiply_fusion = f32[128,4096]{1,0:T(8,128)} fusion(bf16[1024,4096]{1,0:T(8,128)(2,1)} %bitcast.73, f32[1024,128]{1,0:T(8,128)S(1)} %add.165), kind=kOutput, calls=%fused_computation.9 | convolution fusion | flops 1074397184 | bytes 11010048 | tf_op jit(solution)/shard_map/dot_general | solution.py:299
  (174 shorter events, 49.9 us)
Async XLA Ops:
  1.8 85.2 %collective-permute-start.44 = (bf16[128,128]{1,0:T(8,128)(2,1)S(1)}, bf16[128,128]{1,0:T(8,128)(2,1)S(1)}, u32[]{:S(2)}, u32[]{:S(2)}) collective-permute-start(bf16[128,128]{1,0:T(8,128)(2,1)S(1)} %get-tuple-element.50), channel_id=1, source_target_pairs={{3,31},{7,27},{10,22},{14,18},{17,13},{21,9},{24,4},{28,0}} | collective-permute-start | bytes 98312 | tf_op jit(solution)/shard_map/ppermute | solution.py:279
  3.1 80.8 %collective-permute-start.42 = (bf16[128,128]{1,0:T(8,128)(2,1)S(1)}, bf16[128,128]{1,0:T(8,128)(2,1)S(1)}, u32[]{:S(2)}, u32[]{:S(2)}) collective-permute-start(bf16[128,128]{1,0:T(8,128)(2,1)S(1)} %get-tuple-element.51), channel_id=1, source_target_pairs={{2,22},{6,18},{11,31},{15,27},{16,4},{20,0},{25,13},{29,9}} | collective-permute-start | bytes 98312 | tf_op jit(solution)/shard_map/ppermute | solution.py:279
  4.4 29.8 %collective-permute-start.39 = (bf16[128,128]{1,0:T(8,128)(2,1)S(1)}, bf16[128,128]{1,0:T(8,128)(2,1)S(1)}, u32[]{:S(2)}, u32[]{:S(2)}) collective-permute-start(bf16[128,128]{1,0:T(8,128)(2,1)S(1)} %get-tuple-element.54), channel_id=1, source_target_pairs={{1,9},{5,13},{8,0},{12,4},{19,27},{23,31},{26,18},{30,22}} | collective-permute-start | bytes 98312 | tf_op jit(solution)/shard_map/ppermute | solution.py:279
  5.7 25.7 %collective-permute-start.38 = (bf16[128,128]{1,0:T(8,128)(2,1)S(1)}, bf16[128,128]{1,0:T(8,128)(2,1)S(1)}, u32[]{:S(2)}, u32[]{:S(2)}) collective-permute-start(bf16[128,128]{1,0:T(8,128)(2,1)S(1)} %get-tuple-element.55), channel_id=1, source_target_pairs={{2,18},{6,22},{11,27},{15,31},{16,0},{20,4},{25,9},{29,13}} | collective-permute-start | bytes 98312 | tf_op jit(solution)/shard_map/ppermute | solution.py:279
  7.0 21.8 %collective-permute-start.37 = (bf16[128,128]{1,0:T(8,128)(2,1)S(1)}, bf16[128,128]{1,0:T(8,128)(2,1)S(1)}, u32[]{:S(2)}, u32[]{:S(2)}) collective-permute-start(bf16[128,128]{1,0:T(8,128)(2,1)S(1)} %get-tuple-element.56), channel_id=1, source_target_pairs={{0,0},{4,4},{9,9},{13,13},{18,18},{22,22},{27,27},{31,31}} | collective-permute-start | bytes 98312 | tf_op jit(solution)/shard_map/ppermute | solution.py:279
  28.8 8.6 %collective-permute-start.31 = (bf16[128,1024]{1,0:T(8,128)(2,1)S(1)}, bf16[128,1024]{1,0:T(8,128)(2,1)S(1)}, u32[]{:S(2)}, u32[]{:S(2)}) collective-permute-start(bf16[128,1024]{1,0:T(8,128)(2,1)S(1)} %dynamic-slice_convert_fusion.4), channel_id=1, source_target_pairs={{0,1},{1,0},{2,3},{3,2},{4,5},{5,4},{6,7},{7,6},{8,9},{9,8},{10,11... | collective-permute-start | bytes 786440 | tf_op jit(solution)/shard_map/ppermute | solution.py:26
  31.4 56.3 %collective-permute-start.34 = (bf16[1,128,4096]{2,1,0:T(8,128)(2,1)}, bf16[1,128,4096]{2,1,0:T(8,128)(2,1)S(1)}, u32[]{:S(2)}, u32[]{:S(2)}) collective-permute-start(bf16[1,128,4096]{2,1,0:T(8,128)(2,1)} %bitcast.78), channel_id=1, source_target_pairs={{0,16},{4,20},{8,24},{12,28},{16,0},{20,4},{24,8},{28,12},{1,17},{... | collective-permute-start | bytes 3145736 | tf_op jit(solution)/shard_map/ppermute | solution.py:26
  34.2 24.6 %collective-permute-start.41 = (bf16[128,128]{1,0:T(8,128)(2,1)S(1)}, bf16[128,128]{1,0:T(8,128)(2,1)S(1)}, u32[]{:S(2)}, u32[]{:S(2)}) collective-permute-start(bf16[128,128]{1,0:T(8,128)(2,1)S(1)} %get-tuple-element.52), channel_id=1, source_target_pairs={{0,4},{4,0},{9,13},{13,9},{18,22},{22,18},{27,31},{31,27}} | collective-permute-start | bytes 98312 | tf_op jit(solution)/shard_map/ppermute | solution.py:279
  37.4 21.4 %collective-permute-start.40 = (bf16[128,128]{1,0:T(8,128)(2,1)S(1)}, bf16[128,128]{1,0:T(8,128)(2,1)S(1)}, u32[]{:S(2)}, u32[]{:S(2)}) collective-permute-start(bf16[128,128]{1,0:T(8,128)(2,1)S(1)} %get-tuple-element.53), channel_id=1, source_target_pairs={{3,27},{7,31},{10,18},{14,22},{17,9},{21,13},{24,0},{28,4}} | collective-permute-start | bytes 98312 | tf_op jit(solution)/shard_map/ppermute | solution.py:279
  58.8 28.2 %collective-permute-start.43 = (bf16[128,128]{1,0:T(8,128)(2,1)S(1)}, bf16[128,128]{1,0:T(8,128)(2,1)S(1)}, u32[]{:S(2)}, u32[]{:S(2)}) collective-permute-start(bf16[128,128]{1,0:T(8,128)(2,1)S(1)} %get-tuple-element.57), channel_id=1, source_target_pairs={{1,13},{5,9},{8,4},{12,0},{19,31},{23,27},{26,22},{30,18}} | collective-permute-start | bytes 98312 | tf_op jit(solution)/shard_map/ppermute | solution.py:279
  63.8 26.0 %collective-permute-start.9 = (bf16[512,1024]{1,0:T(8,128)(2,1)}, bf16[512,1024]{1,0:T(8,128)(2,1)S(1)}, u32[]{:S(2)}, u32[]{:S(2)}) collective-permute-start(bf16[512,1024]{1,0:T(8,128)(2,1)} %get-tuple-element.24), channel_id=1, source_target_pairs={{0,1},{1,0},{2,3},{3,2},{4,5},{5,4},{6,7},{7,6},{8,9},{9,8},{10,11... | collective-permute-start | bytes 3145736 | tf_op jit(solution)/shard_map/ppermute | solution.py:26
  87.0 8.9 %collective-permute-start.12 = (f32[2,640,256]{2,1,0:T(8,128)}, f32[2,640,256]{2,1,0:T(8,128)S(1)}, u32[]{:S(2)}, u32[]{:S(2)}) collective-permute-start(f32[2,640,256]{2,1,0:T(8,128)} %slice_select_fusion), channel_id=1, source_target_pairs={{0,1},{1,0},{2,3},{3,2},{4,5},{5,4},{6,7},{7,6},{8,9},{9,8},{10,11... | collective-permute-start | bytes 3932168 | tf_op jit(solution)/shard_map/ppermute | solution.py:26
  89.8 84.7 %collective-permute-start.35 = (bf16[2,128,4096]{2,1,0:T(8,128)(2,1)S(1)}, bf16[2,128,4096]{2,1,0:T(8,128)(2,1)S(1)}, u32[]{:S(2)}, u32[]{:S(2)}) collective-permute-start(bf16[2,128,4096]{2,1,0:T(8,128)(2,1)S(1)} %pad_maximum_fusion.4), channel_id=1, source_target_pairs={{0,8},{4,12},{8,0},{12,4},{16,24},{20,28},{24,16},{28,20},{1,9},{5... | collective-permute-start | bytes 6291464 | tf_op jit(solution)/shard_map/ppermute | solution.py:26
  92.3 14.9 %collective-permute-start.10 = (bf16[256,1024]{1,0:T(8,128)(2,1)S(1)}, bf16[256,1024]{1,0:T(8,128)(2,1)S(1)}, u32[]{:S(2)}, u32[]{:S(2)}) collective-permute-start(bf16[256,1024]{1,0:T(8,128)(2,1)S(1)} %dynamic-slice_select_fusion), channel_id=1, source_target_pairs={{0,2},{1,3},{2,0},{3,1},{4,6},{5,7},{6,4},{7,5},{8,10},{9,11},{10,... | collective-permute-start | bytes 1572872 | tf_op jit(solution)/shard_map/ppermute | solution.py:26
  93.3 25.1 %collective-permute-start.7 = (bf16[256,1024]{1,0:T(8,128)(2,1)S(1)}, bf16[256,1024]{1,0:T(8,128)(2,1)S(1)}, u32[]{:S(2)}, u32[]{:S(2)}) collective-permute-start(bf16[256,1024]{1,0:T(8,128)(2,1)S(1)} %dynamic-slice_select_fusion.1), channel_id=1, source_target_pairs={{0,2},{1,3},{2,0},{3,1},{4,6},{5,7},{6,4},{7,5},{8,10},{9,11},{10,... | collective-permute-start | bytes 1572872 | tf_op jit(solution)/shard_map/ppermute | solution.py:26
  94.9 46.0 %collective-permute-start.4 = (bf16[256,1024]{1,0:T(8,128)(2,1)S(1)}, bf16[256,1024]{1,0:T(8,128)(2,1)S(1)}, u32[]{:S(2)}, u32[]{:S(2)}) collective-permute-start(bf16[256,1024]{1,0:T(8,128)(2,1)S(1)} %dynamic-slice_select_fusion.2), channel_id=1, source_target_pairs={{0,2},{1,3},{2,0},{3,1},{4,6},{5,7},{6,4},{7,5},{8,10},{9,11},{10,... | collective-permute-start | bytes 1572872 | tf_op jit(solution)/shard_map/ppermute | solution.py:26
  95.9 45.0 %collective-permute-start.1 = (bf16[256,1024]{1,0:T(8,128)(2,1)S(1)}, bf16[256,1024]{1,0:T(8,128)(2,1)S(1)}, u32[]{:S(2)}, u32[]{:S(2)}) collective-permute-start(bf16[256,1024]{1,0:T(8,128)(2,1)S(1)} %dynamic-slice_select_fusion.3), channel_id=1, source_target_pairs={{0,2},{1,3},{2,0},{3,1},{4,6},{5,7},{6,4},{7,5},{8,10},{9,11},{10,... | collective-permute-start | bytes 1572872 | tf_op jit(solution)/shard_map/ppermute | solution.py:26
  107.2 46.8 %collective-permute-start.13 = (f32[1,640,256]{2,1,0:T(8,128)S(1)}, f32[1,640,256]{2,1,0:T(8,128)S(1)}, u32[]{:S(2)}, u32[]{:S(2)}) collective-permute-start(f32[1,640,256]{2,1,0:T(8,128)S(1)} %slice_select_fusion.1), channel_id=1, source_target_pairs={{0,2},{1,3},{2,0},{3,1},{4,6},{5,7},{6,4},{7,5},{8,10},{9,11},{10,... | collective-permute-start | bytes 1966088 | tf_op jit(solution)/shard_map/ppermute | solution.py:26
  118.4 43.1 %collective-permute-start.11 = (bf16[256,1024]{1,0:T(8,128)(2,1)S(1)}, bf16[256,1024]{1,0:T(8,128)(2,1)S(1)}, u32[]{:S(2)}, u32[]{:S(2)}) collective-permute-start(bf16[256,1024]{1,0:T(8,128)(2,1)S(1)} %broadcast_select_fusion.4), channel_id=1, source_target_pairs={{0,1},{1,0},{2,3},{3,2},{4,5},{5,4},{6,7},{7,6},{8,9},{9,8},{10,11... | collective-permute-start | bytes 1572872 | tf_op jit(solution)/shard_map/ppermute | solution.py:26
  140.9 18.8 %collective-permute-start.8 = (bf16[256,1024]{1,0:T(8,128)(2,1)S(1)}, bf16[256,1024]{1,0:T(8,128)(2,1)S(1)}, u32[]{:S(2)}, u32[]{:S(2)}) collective-permute-start(bf16[256,1024]{1,0:T(8,128)(2,1)S(1)} %broadcast_select_fusion.5), channel_id=1, source_target_pairs={{0,1},{1,0},{2,3},{3,2},{4,5},{5,4},{6,7},{7,6},{8,9},{9,8},{10,11... | collective-permute-start | bytes 1572872 | tf_op jit(solution)/shard_map/ppermute | solution.py:26
  141.0 13.2 %collective-permute-start.2 = (bf16[256,1024]{1,0:T(8,128)(2,1)S(1)}, bf16[256,1024]{1,0:T(8,128)(2,1)S(1)}, u32[]{:S(2)}, u32[]{:S(2)}) collective-permute-start(bf16[256,1024]{1,0:T(8,128)(2,1)S(1)} %broadcast_select_fusion.7), channel_id=1, source_target_pairs={{0,1},{1,0},{2,3},{3,2},{4,5},{5,4},{6,7},{7,6},{8,9},{9,8},{10,11... | collective-permute-start | bytes 1572872 | tf_op jit(solution)/shard_map/ppermute | solution.py:26
  154.1 17.2 %collective-permute-start.14 = (f32[1,640,256]{2,1,0:T(8,128)S(1)}, f32[1,640,256]{2,1,0:T(8,128)S(1)}, u32[]{:S(2)}, u32[]{:S(2)}) collective-permute-start(f32[1,640,256]{2,1,0:T(8,128)S(1)} %select_select_fusion.1), channel_id=1, source_target_pairs={{0,4},{4,0},{8,12},{12,8},{16,20},{20,16},{24,28},{28,24},{1,5},{5... | collective-permute-start | bytes 1966088 | tf_op jit(solution)/shard_map/ppermute | solution.py:26
  155.9 21.2 %collective-permute-start.19 = (bf16[512,1024]{1,0:T(8,128)(2,1)S(1)}, bf16[512,1024]{1,0:T(8,128)(2,1)S(1)}, u32[]{:S(2)}, u32[]{:S(2)}) collective-permute-start(bf16[512,1024]{1,0:T(8,128)(2,1)S(1)} %pad_maximum_fusion.5), channel_id=1, source_target_pairs={{0,16},{4,20},{9,25},{13,29},{18,2},{22,6},{27,11},{31,15}} | collective-permute-start | bytes 3145736 | tf_op jit(solution)/shard_map/ppermute | solution.py:95
  159.7 65.4 %collective-permute-start.22 = (bf16[512,1024]{1,0:T(8,128)(2,1)S(1)}, bf16[512,1024]{1,0:T(8,128)(2,1)S(1)}, u32[]{:S(2)}, u32[]{:S(2)}) collective-permute-start(bf16[512,1024]{1,0:T(8,128)(2,1)S(1)} %pad_maximum_fusion.6), channel_id=1, source_target_pairs={{0,16},{4,20},{9,25},{13,29},{18,2},{22,6},{27,11},{31,15}} | collective-permute-start | bytes 3145736 | tf_op jit(solution)/shard_map/ppermute | solution.py:95
  161.5 66.4 %collective-permute-start.25 = (bf16[512,1024]{1,0:T(8,128)(2,1)S(1)}, bf16[512,1024]{1,0:T(8,128)(2,1)S(1)}, u32[]{:S(2)}, u32[]{:S(2)}) collective-permute-start(bf16[512,1024]{1,0:T(8,128)(2,1)S(1)} %pad_maximum_fusion.7), channel_id=1, source_target_pairs={{0,16},{4,20},{9,25},{13,29},{18,2},{22,6},{27,11},{31,15}} | collective-permute-start | bytes 3145736 | tf_op jit(solution)/shard_map/ppermute | solution.py:95
  171.3 58.4 %collective-permute-start.28 = (bf16[512,1024]{1,0:T(8,128)(2,1)S(1)}, bf16[512,1024]{1,0:T(8,128)(2,1)S(1)}, u32[]{:S(2)}, u32[]{:S(2)}) collective-permute-start(bf16[512,1024]{1,0:T(8,128)(2,1)S(1)} %pad_maximum_fusion.8), channel_id=1, source_target_pairs={{0,16},{4,20},{9,25},{13,29},{18,2},{22,6},{27,11},{31,15}} | collective-permute-start | bytes 3145736 | tf_op jit(solution)/shard_map/ppermute | solution.py:95
  174.5 46.2 %collective-permute-start.15 = (f32[1,640,256]{2,1,0:T(8,128)S(1)}, f32[1,640,256]{2,1,0:T(8,128)S(1)}, u32[]{:S(2)}, u32[]{:S(2)}) collective-permute-start(f32[1,640,256]{2,1,0:T(8,128)S(1)} %broadcast_select_fusion.16), channel_id=1, source_target_pairs={{0,8},{4,12},{8,0},{12,4},{16,24},{20,28},{24,16},{28,20},{1,9},{5... | collective-permute-start | bytes 1966088 | tf_op jit(solution)/shard_map/ppermute | solution.py:26
  177.1 318.5 %collective-permute-start.36 = (bf16[4,128,4096]{2,1,0:T(8,128)(2,1)}, bf16[4,128,4096]{2,1,0:T(8,128)(2,1)}, u32[]{:S(2)}, u32[]{:S(2)}) collective-permute-start(bf16[4,128,4096]{2,1,0:T(8,128)(2,1)} %pad_maximum_fusion.2), channel_id=1, source_target_pairs={{0,4},{4,0},{8,12},{12,8},{16,20},{20,16},{24,28},{28,24},{1,5},{5... | collective-permute-start | bytes 12582920 | tf_op jit(solution)/shard_map/ppermute | solution.py:26
  220.7 37.1 %collective-permute-start.20 = (bf16[512,1024]{1,0:T(8,128)(2,1)S(1)}, bf16[512,1024]{1,0:T(8,128)(2,1)S(1)}, u32[]{:S(2)}, u32[]{:S(2)}) collective-permute-start(bf16[512,1024]{1,0:T(8,128)(2,1)S(1)} %broadcast_select_fusion.3), channel_id=1, source_target_pairs={{0,8},{4,12},{16,24},{20,28},{9,1},{13,5},{25,17},{29,21},{2,10},{... | collective-permute-start | bytes 3145736 | tf_op jit(solution)/shard_map/ppermute | solution.py:95
  225.0 29.5 %collective-permute-start.16 = (f32[1,640,256]{2,1,0:T(8,128)S(1)}, f32[1,640,256]{2,1,0:T(8,128)S(1)}, u32[]{:S(2)}, u32[]{:S(2)}) collective-permute-start(f32[1,640,256]{2,1,0:T(8,128)S(1)} %broadcast_select_fusion.17), channel_id=1, source_target_pairs={{0,16},{4,20},{8,24},{12,28},{16,0},{20,4},{24,8},{28,12},{1,17},{... | collective-permute-start | bytes 1966088 | tf_op jit(solution)/shard_map/ppermute | solution.py:26
  228.0 54.3 %collective-permute-start.23 = (bf16[512,1024]{1,0:T(8,128)(2,1)S(1)}, bf16[512,1024]{1,0:T(8,128)(2,1)S(1)}, u32[]{:S(2)}, u32[]{:S(2)}) collective-permute-start(bf16[512,1024]{1,0:T(8,128)(2,1)S(1)} %broadcast_select_fusion.2), channel_id=1, source_target_pairs={{0,8},{4,12},{16,24},{20,28},{9,1},{13,5},{25,17},{29,21},{2,10},{... | collective-permute-start | bytes 3145736 | tf_op jit(solution)/shard_map/ppermute | solution.py:95
  229.8 53.8 %collective-permute-start.26 = (bf16[512,1024]{1,0:T(8,128)(2,1)S(1)}, bf16[512,1024]{1,0:T(8,128)(2,1)S(1)}, u32[]{:S(2)}, u32[]{:S(2)}) collective-permute-start(bf16[512,1024]{1,0:T(8,128)(2,1)S(1)} %broadcast_select_fusion.1), channel_id=1, source_target_pairs={{0,8},{4,12},{16,24},{20,28},{9,1},{13,5},{25,17},{29,21},{2,10},{... | collective-permute-start | bytes 3145736 | tf_op jit(solution)/shard_map/ppermute | solution.py:95
  254.5 30.1 %collective-permute-start.29 = (bf16[512,1024]{1,0:T(8,128)(2,1)S(1)}, bf16[512,1024]{1,0:T(8,128)(2,1)S(1)}, u32[]{:S(2)}, u32[]{:S(2)}) collective-permute-start(bf16[512,1024]{1,0:T(8,128)(2,1)S(1)} %broadcast_select_fusion), channel_id=1, source_target_pairs={{0,8},{4,12},{16,24},{20,28},{9,1},{13,5},{25,17},{29,21},{2,10},{... | collective-permute-start | bytes 3145736 | tf_op jit(solution)/shard_map/ppermute | solution.py:95
  257.8 32.9 %collective-permute-start.17 = (f32[1,640,256]{2,1,0:T(8,128)S(1)}, f32[1,640,256]{2,1,0:T(8,128)S(1)}, u32[]{:S(2)}, u32[]{:S(2)}) collective-permute-start(f32[1,640,256]{2,1,0:T(8,128)S(1)} %broadcast_select_fusion.18), channel_id=1, source_target_pairs={{0,2},{1,3},{2,0},{3,1},{4,6},{5,7},{6,4},{7,5},{8,10},{9,11},{10,... | collective-permute-start | bytes 1966088 | tf_op jit(solution)/shard_map/ppermute | solution.py:26
  282.2 54.0 %collective-permute-start.21 = (bf16[1,512,1024]{2,1,0:T(8,128)(2,1)S(1)}, bf16[1,512,1024]{2,1,0:T(8,128)(2,1)S(1)}, u32[]{:S(2)}, u32[]{:S(2)}) collective-permute-start(bf16[1,512,1024]{2,1,0:T(8,128)(2,1)S(1)} %select_bitcast_fusion.13), channel_id=1, source_target_pairs={{0,4},{4,0},{8,12},{12,8},{16,20},{20,16},{24,28},{28,24},{1,5},{5... | collective-permute-start | bytes 3145736 | tf_op jit(solution)/shard_map/ppermute | solution.py:26
  283.5 75.1 %collective-permute-start.24 = (bf16[1,512,1024]{2,1,0:T(8,128)(2,1)S(1)}, bf16[1,512,1024]{2,1,0:T(8,128)(2,1)S(1)}, u32[]{:S(2)}, u32[]{:S(2)}) collective-permute-start(bf16[1,512,1024]{2,1,0:T(8,128)(2,1)S(1)} %select_bitcast_fusion.10), channel_id=1, source_target_pairs={{0,4},{4,0},{8,12},{12,8},{16,20},{20,16},{24,28},{28,24},{1,5},{5... | collective-permute-start | bytes 3145736 | tf_op jit(solution)/shard_map/ppermute | solution.py:26
  284.6 96.5 %collective-permute-start.27 = (bf16[1,512,1024]{2,1,0:T(8,128)(2,1)S(1)}, bf16[1,512,1024]{2,1,0:T(8,128)(2,1)S(1)}, u32[]{:S(2)}, u32[]{:S(2)}) collective-permute-start(bf16[1,512,1024]{2,1,0:T(8,128)(2,1)S(1)} %select_bitcast_fusion.7), channel_id=1, source_target_pairs={{0,4},{4,0},{8,12},{12,8},{16,20},{20,16},{24,28},{28,24},{1,5},{5... | collective-permute-start | bytes 3145736 | tf_op jit(solution)/shard_map/ppermute | solution.py:26
  290.7 112.5 %collective-permute-start.30 = (bf16[1,512,1024]{2,1,0:T(8,128)(2,1)S(1)}, bf16[1,512,1024]{2,1,0:T(8,128)(2,1)S(1)}, u32[]{:S(2)}, u32[]{:S(2)}) collective-permute-start(bf16[1,512,1024]{2,1,0:T(8,128)(2,1)S(1)} %select_bitcast_fusion.4), channel_id=1, source_target_pairs={{0,4},{4,0},{8,12},{12,8},{16,20},{20,16},{24,28},{28,24},{1,5},{5... | collective-permute-start | bytes 3145736 | tf_op jit(solution)/shard_map/ppermute | solution.py:26
  336.2 71.3 %collective-permute-start.18 = (f32[2,640,256]{2,1,0:T(8,128)S(1)}, f32[2,640,256]{2,1,0:T(8,128)S(1)}, u32[]{:S(2)}, u32[]{:S(2)}) collective-permute-start(f32[2,640,256]{2,1,0:T(8,128)S(1)} %maximum_bitcast_fusion.4), channel_id=1, source_target_pairs={{0,1},{1,0},{2,3},{3,2},{4,5},{5,4},{6,7},{7,6},{8,9},{9,8},{10,11... | collective-permute-start | bytes 3932168 | tf_op jit(solution)/shard_map/ppermute | solution.py:26
  504.8 15.6 %collective-permute-start.46 = (f32[1024,128]{1,0:T(8,128)S(1)}, f32[1024,128]{1,0:T(8,128)S(1)}, u32[]{:S(2)}, u32[]{:S(2)}) collective-permute-start(f32[1024,128]{1,0:T(8,128)S(1)} %add.164), channel_id=1, source_target_pairs={{0,2},{1,3},{2,0},{3,1},{4,6},{5,7},{6,4},{7,5},{8,10},{9,11},{10,... | collective-permute-start | bytes 1572872 | tf_op jit(solution)/shard_map/ppermute | solution.py:26
  520.5 44.8 %collective-permute-start.47 = (f32[128,128]{1,0:T(8,128)S(1)}, f32[128,128]{1,0:T(8,128)S(1)}, u32[]{:S(2)}, u32[]{:S(2)}) collective-permute-start(f32[128,128]{1,0:T(8,128)S(1)} %get-tuple-element.40), channel_id=1, source_target_pairs={{0,0},{4,4},{9,9},{13,13},{18,18},{22,22},{27,27},{31,31}} | collective-permute-start | bytes 196616 | tf_op jit(solution)/shard_map/ppermute | solution.py:306
  521.2 45.4 %collective-permute-start.54 = (f32[128,128]{1,0:T(8,128)S(1)}, f32[128,128]{1,0:T(8,128)S(1)}, u32[]{:S(2)}, u32[]{:S(2)}) collective-permute-start(f32[128,128]{1,0:T(8,128)S(1)} %get-tuple-element.41), channel_id=1, source_target_pairs={{0,28},{4,24},{9,21},{13,17},{18,14},{22,10},{27,7},{31,3}} | collective-permute-start | bytes 196616 | tf_op jit(solution)/shard_map/ppermute | solution.py:306
  526.5 41.4 %collective-permute-start.53 = (f32[128,128]{1,0:T(8,128)S(1)}, f32[128,128]{1,0:T(8,128)S(1)}, u32[]{:S(2)}, u32[]{:S(2)}) collective-permute-start(f32[128,128]{1,0:T(8,128)S(1)} %get-tuple-element.42), channel_id=1, source_target_pairs={{0,12},{4,8},{9,5},{13,1},{18,30},{22,26},{27,23},{31,19}} | collective-permute-start | bytes 196616 | tf_op jit(solution)/shard_map/ppermute | solution.py:306
  560.6 14.6 %collective-permute-start.52 = (f32[128,128]{1,0:T(8,128)S(1)}, f32[128,128]{1,0:T(8,128)S(1)}, u32[]{:S(2)}, u32[]{:S(2)}) collective-permute-start(f32[128,128]{1,0:T(8,128)S(1)} %get-tuple-element.43), channel_id=1, source_target_pairs={{0,20},{4,16},{9,29},{13,25},{18,6},{22,2},{27,15},{31,11}} | collective-permute-start | bytes 196616 | tf_op jit(solution)/shard_map/ppermute | solution.py:306
  561.9 13.3 %collective-permute-start.51 = (f32[128,128]{1,0:T(8,128)S(1)}, f32[128,128]{1,0:T(8,128)S(1)}, u32[]{:S(2)}, u32[]{:S(2)}) collective-permute-start(f32[128,128]{1,0:T(8,128)S(1)} %get-tuple-element.44), channel_id=1, source_target_pairs={{0,4},{4,0},{9,13},{13,9},{18,22},{22,18},{27,31},{31,27}} | collective-permute-start | bytes 196616 | tf_op jit(solution)/shard_map/ppermute | solution.py:306
  565.3 9.9 %collective-permute-start.50 = (f32[128,128]{1,0:T(8,128)S(1)}, f32[128,128]{1,0:T(8,128)S(1)}, u32[]{:S(2)}, u32[]{:S(2)}) collective-permute-start(f32[128,128]{1,0:T(8,128)S(1)} %get-tuple-element.45), channel_id=1, source_target_pairs={{0,24},{4,28},{9,17},{13,21},{18,10},{22,14},{27,3},{31,7}} | collective-permute-start | bytes 196616 | tf_op jit(solution)/shard_map/ppermute | solution.py:306
  566.6 8.6 %collective-permute-start.49 = (f32[128,128]{1,0:T(8,128)S(1)}, f32[128,128]{1,0:T(8,128)S(1)}, u32[]{:S(2)}, u32[]{:S(2)}) collective-permute-start(f32[128,128]{1,0:T(8,128)S(1)} %get-tuple-element.46), channel_id=1, source_target_pairs={{0,8},{4,12},{9,1},{13,5},{18,26},{22,30},{27,19},{31,23}} | collective-permute-start | bytes 196616 | tf_op jit(solution)/shard_map/ppermute | solution.py:306
  567.9 7.3 %collective-permute-start.48 = (f32[128,128]{1,0:T(8,128)S(1)}, f32[128,128]{1,0:T(8,128)S(1)}, u32[]{:S(2)}, u32[]{:S(2)}) collective-permute-start(f32[128,128]{1,0:T(8,128)S(1)} %get-tuple-element.47), channel_id=1, source_target_pairs={{0,16},{4,20},{9,25},{13,29},{18,2},{22,6},{27,11},{31,15}} | collective-permute-start | bytes 196616 | tf_op jit(solution)/shard_map/ppermute | solution.py:306
  (19 other events, 206.4 us)

commit v2 on v1

v2 whole, which is shorter than its diff:
```python
import functools
import math

import jax
import jax.numpy as jnp
from jax import lax
from jax.experimental import pallas as pl
from jax.experimental.pallas import tpu as pltpu
from jax.sharding import PartitionSpec as P

PW = 1024
TILE = 256
COLS = 512
ROWS = 256
NB = 128
GROUPS = 8

BF16 = jnp.bfloat16
F32 = jnp.float32


def bits(n):
    return [1 << b for b in range(n.bit_length() - 1)]


def swap(x, axis, bit):
    n = lax.axis_size(axis)
    return lax.ppermute(x, axis, [(i, i ^ bit) for i in range(n)])


def joint(pairs, cols):
    return [(a * cols + c, b * cols + d) for (a, c), (b, d) in pairs]


def pick(cond, a, b):
    return jnp.where(cond, a, b), jnp.where(cond, b, a)


def scatter(x, root, bit):
    col = lax.axis_index("col")
    mine, other = pick((col & bit) == 0, x[0::2], x[1::2])
    return jnp.where(((col ^ root) & bit) == 0, mine, swap(other, "col", bit))


def join(x, got, bit):
    a, b = pick((lax.axis_index("col") & bit) == 0, x, got)
    return jnp.stack([a, b], 1).reshape((2 * x.shape[0],) + x.shape[1:])


def rotated(d, n):
    return (d * 2) % n + d * 2 // n


def transpose_parts(x):
    n_row, n_col = lax.axis_size("row"), lax.axis_size("col")
    k = n_row // n_col
    pairs = [
        ((c * k + lo, rotated(d, n_col)), (d * k + lo, c))
        for c in range(n_col)
        for d in range(n_col)
        for lo in range(k)
    ]
    return lax.ppermute(x, ("row", "col"), joint(pairs, n_col))


def gate(*arrays):
    flat, tree = jax.tree.flatten(arrays)
    free = [pl.BlockSpec(memory_space=pl.ANY)] * len(flat)
    flat = pl.pallas_call(
        lambda *refs: None,
        out_shape=[jax.ShapeDtypeStruct(x.shape, x.dtype) for x in flat],
        in_specs=free,
        out_specs=free,
        input_output_aliases={i: i for i in range(len(flat))},
    )(*flat)
    return jax.tree.unflatten(tree, flat)


def spread_block(block, owner_row, owner_col):
    row, col = lax.axis_index("row"), lax.axis_index("col")
    col_bits, row_bits = bits(lax.axis_size("col")), bits(lax.axis_size("row"))
    for bit in col_bits:
        block = scatter(block, owner_col, bit)
    for bit in row_bits[-1:] + row_bits[:-1]:
        block = jnp.where(((row ^ owner_row) & bit) == 0, block, swap(block, "row", bit))
    for bit in reversed(col_bits):
        block = join(block, swap(block, "col", bit), bit)
    return block


def gather_rows(x):
    *near, far = bits(lax.axis_size("row"))
    parts = {0: x, far: swap(x, "row", far)}
    for root in (0, far):
        level = [root]
        for bit in reversed(near):
            parts.update({i ^ bit: swap(parts[i], "row", bit) for i in level})
            level = level + [i ^ bit for i in level]
    return parts


def assemble(parts, start):
    rows, cols = parts[0].shape
    out = jnp.zeros((rows * len(parts), cols), parts[0].dtype)
    for i, part in parts.items():
        out = lax.dynamic_update_slice_in_dim(out, part, start(lax.axis_index("row") ^ i), 0)
    return out


def dot32(a, b):
    ah, bh = a.astype(BF16), b.astype(BF16)
    al, bl = (a - ah.astype(F32)).astype(BF16), (b - bh.astype(F32)).astype(BF16)
    dot = functools.partial(jnp.dot, preferred_element_type=F32)
    return dot(ah, bh) + (dot(ah, bl) + dot(al, bh))


def wide(x, n):
    return jnp.broadcast_to(x, (x.shape[0], n))


def sweep_panel(t, k, lane, sub):
    n = t.shape[1]
    for j in range(0, 8, 2):
        c0, c1 = wide(t[:, k + j : k + j + 1], n), wide(t[:, k + j + 1 : k + j + 2], n)
        r0, r1 = t[j : j + 1, :], t[j + 1 : j + 2, :]
        p, q = c0[j : j + 1, :], c1[j : j + 1, :]
        q2, s = c0[j + 1 : j + 2, :], c1[j + 1 : j + 2, :]
        inv = 1.0 / (p * s - q * q2)
        on0, on1 = lane == k + j, lane == k + j + 1
        b0 = jnp.where(on0, 1.0, jnp.where(on1, 0.0, r0))
        b1 = jnp.where(on0, 0.0, jnp.where(on1, 1.0, r1))
        e0 = (s * b0 - q * b1) * inv
        e1 = (p * b1 - q2 * b0) * inv
        a0 = jnp.where(on0, e0 + 1.0, e0)
        a1 = jnp.where(on1, e1 + 1.0, e1)
        u = t - c0 * a0 - c1 * a1
        t = jnp.where(sub == j, e0, jnp.where(sub == j + 1, e1, u))
    return t


def sweep(t):
    n = t[0].shape[1]
    lane = lax.broadcasted_iota(jnp.int32, (1, n), 1)
    sub = lax.broadcasted_iota(jnp.int32, (8, n), 0)
    t = list(t)
    count = len(t)
    for at in range(count):
        k = 8 * at
        new = sweep_panel(t[at], k, lane, sub)
        inside = (lane >= k) & (lane < k + 8)
        rows = [jnp.broadcast_to(new[j : j + 1, :], (8, n)) for j in range(8)]
        for i in [(at + 1 + step) % count for step in range(count - 1)]:
            u = jnp.where(inside, 0.0, t[i])
            for j in range(8):
                u = u - wide(t[i][:, k + j : k + j + 1], n) * rows[j]
            t[i] = u
        t[at] = new
    return t


def inverse_kernel(first, groups, *refs):
    a_ref = refs[-1]
    n = a_ref.shape[0]
    if first == 0:
        packed_ref = refs[0]
        at = 0
        for i in range(n // TILE):
            for j in range(i + 1):
                part = packed_ref[at * TILE : (at + 1) * TILE, :]
                a_ref[i * TILE : (i + 1) * TILE, j * TILE : (j + 1) * TILE] = part
                if i != j:
                    a_ref[j * TILE : (j + 1) * TILE, i * TILE : (i + 1) * TILE] = part.T
                at += 1
    else:
        a_ref[...] = refs[0][...]
    eye = (
        lax.broadcasted_iota(jnp.int32, (NB, NB), 0) == lax.broadcasted_iota(jnp.int32, (NB, NB), 1)
    ).astype(F32)

    def step(k, _):
        o = pl.multiple_of(k * NB, NB)
        t = [
            a_ref[pl.ds(pl.multiple_of(o + 8 * i, 8), 8), pl.ds(o, NB)] for i in range(NB // 8)
        ]
        pivot = jnp.concatenate(sweep(t), 0)
        a_ref[pl.ds(o, NB), pl.ds(o, NB)] = eye
        new = dot32(pivot, a_ref[pl.ds(o, NB), :])

        def update(i, _):
            r = pl.multiple_of(i * TILE, TILE)
            c = a_ref[pl.ds(r, TILE), pl.ds(o, NB)]
            a_ref[pl.ds(r, TILE), pl.ds(o, NB)] = jnp.zeros((TILE, NB), F32)
            a_ref[pl.ds(r, TILE), :] = a_ref[pl.ds(r, TILE), :] - dot32(c, new)
            return 0

        lax.fori_loop(0, n // TILE, update, 0)
        a_ref[pl.ds(o, NB), :] = new
        return 0

    count = n // NB // groups
    lax.fori_loop(first * count, (first + 1) * count, step, 0)

    if first == groups - 1:
        high_ref, low_ref = refs[1:3]

        def store(i, _):
            r = pl.multiple_of(i * NB, NB)
            a = a_ref[pl.ds(r, NB), :]
            high = a.astype(BF16)
            high_ref[pl.ds(r, NB), :] = high
            low_ref[pl.ds(r, NB), :] = (a - high.astype(F32)).astype(BF16)
            return 0

        lax.fori_loop(0, n // NB, store, 0)


def inverse_call(first, state):
    vmem = pl.BlockSpec(memory_space=pltpu.VMEM)
    last = first == GROUPS - 1
    count = 2 if last else 1
    out = [jax.ShapeDtypeStruct((PW, PW), BF16 if last else F32)] * count
    state = pl.pallas_call(
        functools.partial(inverse_kernel, first, GROUPS),
        out_shape=out,
        in_specs=[vmem],
        out_specs=[vmem] * count,
        scratch_shapes=[pltpu.VMEM((PW, PW), F32)] if last else [],
        compiler_params=pltpu.CompilerParams(vmem_limit_bytes=24 << 20),
        cost_estimate=pl.CostEstimate(
            flops=80 * PW**3 // GROUPS, bytes_accessed=8 * PW**2, transcendentals=0
        ),
    )(state)
    return state if last else state[0]


def pack_kernel(place_ref, inverse_ref, out_ref, sems):
    row, col = pl.multiple_of(place_ref[0], TILE), pl.multiple_of(place_ref[1], TILE)
    copies = []
    for i in range(PW // TILE):
        for j in range(i + 1):
            at = len(copies)
            copies.append(
                pltpu.make_async_copy(
                    inverse_ref.at[pl.ds(row + i * TILE, TILE), pl.ds(col + j * TILE, TILE)],
                    out_ref.at[pl.ds(at * TILE, TILE), :],
                    sems.at[at],
                )
            )
    for copy in copies:
        copy.start()
    for copy in copies:
        copy.wait()


def pack(inverse, row, col):
    count = (PW // TILE) * (PW // TILE + 1) // 2
    return pl.pallas_call(
        pack_kernel,
        out_shape=jax.ShapeDtypeStruct((count * TILE, TILE), F32),
        in_specs=[pl.BlockSpec(memory_space=pltpu.SMEM), pl.BlockSpec(memory_space=pl.ANY)],
        out_specs=pl.BlockSpec(memory_space=pltpu.VMEM),
        scratch_shapes=[pltpu.SemaphoreType.DMA((count,))],
    )(jnp.stack([row, col]).astype(jnp.int32), inverse)


def nt(a, b):
    return lax.dot_general(a, b, (((1,), (1,)), ((), ())), preferred_element_type=F32)


def nn(a, b):
    return lax.dot_general(a, b, (((1,), (0,)), ((), ())), preferred_element_type=F32)


def pruned_kernel(weight_ref, mixed_ref, panel_ref, pruned_ref, pruned_low_ref):
    step = min(COLS, weight_ref.shape[1])
    for at in range(0, weight_ref.shape[1], step):
        pruned = weight_ref[:, at : at + step] - nt(mixed_ref[...], panel_ref[at : at + step, :])
        pruned_ref[:, at : at + step] = pruned
        pruned_low_ref[:, at : at + step] = pruned.astype(BF16)


def remove_from_weight(weight, mixed, panel):
    vmem = pl.BlockSpec(memory_space=pltpu.VMEM)
    rows, cols = weight.shape
    return pl.pallas_call(
        pruned_kernel,
        out_shape=(
            jax.ShapeDtypeStruct((rows, cols), F32),
            jax.ShapeDtypeStruct((rows, cols), BF16),
        ),
        in_specs=[vmem] * 3,
        out_specs=(vmem, vmem),
        compiler_params=pltpu.CompilerParams(vmem_limit_bytes=40 << 20),
        cost_estimate=pl.CostEstimate(
            flops=2 * rows * PW * cols, bytes_accessed=2 * PW * cols, transcendentals=0
        ),
    )(weight, mixed, panel)


def inverse_step_kernel(inverse_ref, mixed_ref, panel_ref, *refs):
    out_ref = refs[-1]
    step = min(COLS, inverse_ref.shape[1])
    for at in range(0, inverse_ref.shape[1], step):
        change = nt(mixed_ref[...], panel_ref[at : at + step, :])
        out_ref[:, at : at + step] = inverse_ref[:, at : at + step] - change


def remove_from_inverse(half, inverse, mixed, panel, done=None):
    vmem = pl.BlockSpec(memory_space=pltpu.VMEM)
    rows, cols = inverse.shape
    step = min(ROWS, rows // 2)
    count = rows // 2 // step
    base = half * count
    return pl.pallas_call(
        inverse_step_kernel,
        grid=(count,),
        out_shape=jax.ShapeDtypeStruct((rows, cols), F32),
        in_specs=[
            pl.BlockSpec((step, cols), lambda i: (base + i, 0)),
            pl.BlockSpec((step, PW), lambda i: (base + i, 0)),
            vmem,
        ]
        + [pl.BlockSpec(memory_space=pl.ANY)] * half,
        out_specs=pl.BlockSpec((step, cols), lambda i: (base + i, 0)),
        input_output_aliases={3: 0} if half else {},
        compiler_params=pltpu.CompilerParams(vmem_limit_bytes=52 << 20),
        cost_estimate=pl.CostEstimate(
            flops=rows * PW * cols, bytes_accessed=4 * rows * cols, transcendentals=0
        ),
    )(inverse, mixed, panel, *([done] if half else []))


def shards(panels, inverse, weight, tokens, targets):
    n_row, n_col = lax.axis_size("row"), lax.axis_size("col")
    k = n_row // n_col
    row, col = lax.axis_index("row"), lax.axis_index("col")
    rows_local, cols_local = inverse.shape
    out_rows = weight.shape[0]
    token_rows = tokens.shape[0]
    anchor = panels[0] * PW
    owner_col, col_offset = anchor // cols_local, anchor % cols_local
    owner_row, row_offset = anchor // rows_local, anchor % rows_local

    block = pack(inverse, row_offset, col_offset).reshape(n_col, -1, TILE)
    block = spread_block(block, owner_row, owner_col).reshape(-1, TILE)
    tiled = targets.reshape(token_rows, k, out_rows).swapaxes(0, 1)
    tiled = jnp.concatenate([tiled] * n_col, 0)
    state, tiled = gate(block, tiled)

    size, weight_size = rows_local // n_col, out_rows // n_col
    slab = lax.dynamic_slice_in_dim(inverse, col_offset, PW, 1).astype(BF16)
    weight_slab = lax.dynamic_slice_in_dim(weight, col_offset, PW, 1).astype(BF16)
    slab = jnp.concatenate(
        [slab.reshape(n_col, size, PW), weight_slab.reshape(n_col, weight_size, PW)], 1
    )
    for bit in bits(n_col):
        slab = scatter(slab, owner_col, bit)
    panel = gather_rows(transpose_parts(slab[0, :size]))
    panel = assemble(panel, lambda r: (r % k) * rows_local + rotated(r // k, n_col) * size)
    for bit in reversed(bits(n_col)):
        slab = join(slab, swap(slab, "col", bit), bit)
    column = slab[:, :size].reshape(rows_local, PW)
    weight_slab = slab[:, size:].reshape(out_rows, PW)

    all_tokens = assemble(gather_rows(tokens), lambda r: r * token_rows)
    value_targets = lax.all_to_all(tiled, "row", 0, 0).reshape(-1, out_rows)

    for first in range(GROUPS):
        state = inverse_call(first, state)
    high, low = state
    both = jnp.concatenate([high, low], 0)
    mixed = nn(jnp.concatenate([column, column], 1), both)
    place = lax.broadcasted_iota(jnp.int32, mixed.shape, 0) - row_offset
    unit = (place == lax.broadcasted_iota(jnp.int32, mixed.shape, 1)).astype(F32)
    inside = (row == owner_row) & (place >= 0) & (place < PW)
    mixed = jnp.where(inside, unit, mixed).astype(BF16)
    mixed_weight = nn(jnp.concatenate([weight_slab, weight_slab], 1), both).astype(BF16)

    pruned, pruned_low = remove_from_weight(weight, mixed_weight, panel)

    value_targets = jnp.where(col == row // k, value_targets.astype(F32), 0.0)
    value = nt(all_tokens, pruned_low) - value_targets
    new_inverse = remove_from_inverse(0, inverse, mixed, panel)
    for bit in bits(n_col):
        value = value + swap(value, "col", bit)
    value, new_inverse = lax.optimization_barrier((value, new_inverse))
    value_low = value.astype(BF16)
    correlation = lax.dot_general(
        value_low, all_tokens, (((0,), (0,)), ((), ())), preferred_element_type=F32
    ) * (1.0 / math.sqrt(token_rows * n_row))

    tiles = lax.all_to_all(value.reshape(n_row, token_rows, out_rows), "row", 0, 0)
    tiles = lax.dynamic_slice_in_dim(tiles, col * k, k, 0)
    residual = jnp.concatenate([tiles[lo] for lo in range(k)], 1)

    new_inverse = remove_from_inverse(1, inverse, mixed, panel, new_inverse)
    return (new_inverse, pruned, residual, correlation)


def solution(mesh):
    in_specs = (P(), P("row", "col"), P("row", "col"), P("row", "col"), P("row", "col"))
    out_specs = (P("row", "col"), P("row", "col"), P("row", "col"), P("row", "col"))
    return jax.shard_map(shards, mesh=mesh, in_specs=in_specs, out_specs=out_specs, check_vma=False)
```

time: 585 us -> 423 us (0.72)
  waiting for transfers between devices: 230 us -> 121 us
  starting transfers between devices: 158 us -> 77.9 us
  Pallas kernels: 75.2 us -> 124 us
  matrix products: 65.3 us -> 28 us
  local copies, waits for them, and re-layouts: 23.6 us -> 47.3 us
    ppermute x31 -> x27, waiting for transfers between devices: 206 us -> 121 us  [swap(): return lax.ppermute(x, axis, [(i, i ^ bit) for i in range(n)])]
    pallas_call x1 -> x13, Pallas kernels: 75.2 us -> 124 us  [the longest x8 77.3 us: inverse_call(): pl.pallas_call(functools.partial(inverse_kernel, first, GROUPS), out_shap...]
    ppermute x24 -> x1, starting transfers between devices: 46.4 us -> 0.94 us  [transpose_parts(): return lax.ppermute(x, ('row', 'col'), joint(pairs, n_col))]
    ppermute x31 -> x27, starting transfers between devices: 112 us -> 66.6 us  [swap(): return lax.ppermute(x, axis, [(i, i ^ bit) for i in range(n)])]
    dot_general x3 -> x1, matrix products: 45.2 us -> 5.71 us  [nt(): lax.dot_general(a, b, (((1,), (1,)), ((), ())), preferred_element_type=F32)]
    ppermute x24 -> x1, waiting for transfers between devices: 23.1 us -> 0.01 us  [transpose_parts(): return lax.ppermute(x, ('row', 'col'), joint(pairs, n_col))]
    dynamic_update_slice x0 -> x16, local copies, waits for them, and re-layouts: none -> 22.1 us  [assemble(): lax.dynamic_update_slice_in_dim(out, part, start(lax.axis_index('row') ^...]
    all_to_all x0 -> x2, starting transfers between devices: none -> 10.3 us  [the longest x1 5.89 us: shards(): lax.all_to_all(value.reshape(n_row, token_rows, out_rows), 'row', 0, 0)]
  transfers between devices with their start and end apart: 55 -> 30, of which waited for: 16 -> 7; matrix products, arithmetic and copies ran while one was open for 17% -> 18% of each run, Pallas kernels for 13% -> 29%
where the time goes in v2:
time: 423 us; the launch traced here: 417 us
  Pallas kernels  124 us (29%)
  waiting for transfers between devices  121 us (29%)
  starting transfers between devices  77.9 us (18%)
  local copies, waits for them, and re-layouts  47.3 us (11%)
  matrix products  28 us (7%)
  other arithmetic  16.9 us (4%)
    ppermute x27, waiting for transfers between devices, swap(): return lax.ppermute(x, axis, [(i, i ^ bit) for i in range(n)])  121 us
    pallas_call x8, Pallas kernels, inverse_call(): pl.pallas_call(functools.partial(inverse_kernel, first, GROUPS), out_shap...  77.3 us
    ppermute x27, starting transfers between devices, swap(): return lax.ppermute(x, axis, [(i, i ^ bit) for i in range(n)])  66.6 us
    pallas_call x2, Pallas kernels, remove_from_inverse(): pl.pallas_call(inverse_step_kernel, grid=(count,), out_shape=jax.ShapeDty...  38.3 us
    dynamic_update_slice x16, local copies, waits for them, and re-layouts, assemble(): lax.dynamic_update_slice_in_dim(out, part, start(lax.axis_index('row') ^...  22.1 us
    dot_general x2, matrix products, nn(): lax.dot_general(a, b, (((1,), (0,)), ((), ())), preferred_element_type=F32)  16.1 us
    unnamed x32, local copies, waits for them, and re-layouts  11.7 us
  transfers between devices with their start and end apart: 30, of which 7 were waited for; matrix products, arithmetic and copies ran while one was open for 18% of the time, Pallas kernels for 29%

profile of v2, /device:TPU:0, one launch (start us, length us, event | category | flops | bytes accessed | tf_op | source)
XLA Modules:
  0.0 417.1 jit_solution(11136166747112815624)
XLA Ops:
  0.6 4.1 collective-permute-start.19
  9.1 4.0 shard_map.84
  13.0 1.9 slice_select_fusion
  15.0 5.3 %dynamic-slice_convert_fusion = bf16[2048,1024]{1,0:T(8,128)(2,1)S(1)} fusion(f32[2048,4096]{1,0:T(8,128)} %inverse_ref.5, s32[]{:T(128)S(6)} %select_n.331), kind=kLoop, calls=%fused_computation.5 | loop fusion | bytes 8388612 | tf_op jit(solution)/shard_map/convert_element_type | solution.py:351
  21.0 2.1 copy-done.6
  25.2 4.3 %broadcast_in_dim.11 = bf16[1024,4096]{1,0:T(8,128)(2,1)} broadcast(bf16[]{:T(256)} %constant.263.clone.1), dimensions={} | broadcast | bytes 8388610 | tf_op jit(solution)/shard_map/broadcast_in_dim | solution.py:104
  31.1 2.1 select_select_fusion.1
  35.6 15.3 %collective-permute-done.20 = bf16[128,4096]{1,0:T(8,128)(2,1)} collective-permute-done((bf16[128,4096]{1,0:T(8,128)(2,1)}, bf16[128,4096]{1,0:T(8,128)(2,1)}, u32[]{:S(2)}, u32[]{:S(2)}) %collective-permute-start.20) | collective-permute-done | bytes 1048608 | tf_op jit(solution)/shard_map/ppermute | solution.py:28
  54.0 2.3 constant_dynamic-update-slice_fusion.8
  57.4 2.3 constant_dynamic-update-slice_fusion.7
  61.7 27.8 %collective-permute-done.6 = f32[1,640,256]{2,1,0:T(8,128)S(1)} collective-permute-done((f32[1,640,256]{2,1,0:T(8,128)S(1)}, f32[1,640,256]{2,1,0:T(8,128)S(1)}, u32[]{:S(2)}, u32[]{:S(2)}) %collective-permute-start.6) | collective-permute-done | bytes 655392 | tf_op jit(solution)/shard_map/ppermute | solution.py:28
  91.9 2.3 constant_dynamic-update-slice_fusion.6
  95.7 18.1 %collective-permute-done.7 = f32[1,640,256]{2,1,0:T(8,128)S(1)} collective-permute-done((f32[1,640,256]{2,1,0:T(8,128)S(1)}, f32[1,640,256]{2,1,0:T(8,128)S(1)}, u32[]{:S(2)}, u32[]{:S(2)}) %collective-permute-start.7) | collective-permute-done | bytes 655392 | tf_op jit(solution)/shard_map/ppermute | solution.py:28
  117.7 25.0 %collective-permute-done.8 = f32[1,640,256]{2,1,0:T(8,128)S(1)} collective-permute-done((f32[1,640,256]{2,1,0:T(8,128)S(1)}, f32[1,640,256]{2,1,0:T(8,128)S(1)}, u32[]{:S(2)}, u32[]{:S(2)}) %collective-permute-start.8) | collective-permute-done | bytes 655392 | tf_op jit(solution)/shard_map/ppermute | solution.py:28
  143.9 2.0 collective-permute-start.2
  146.9 20.7 %collective-permute-start.12 = (bf16[512,1024]{1,0:T(8,128)(2,1)S(1)}, bf16[512,1024]{1,0:T(8,128)(2,1)}, u32[]{:S(2)}, u32[]{:S(2)}) collective-permute-start(bf16[512,1024]{1,0:T(8,128)(2,1)S(1)} %collective-permute-done.11), channel_id=1, source_target_pairs={{0,16},{4,20},{8,24},{12,28},{16,0},{20,4},{24,8},{28,12},{1,17},{... | collective-permute-start | bytes 3145736 | tf_op jit(solution)/shard_map/ppermute | solution.py:28
  167.7 2.5 collective-permute-start.13
  174.6 8.7 %collective-permute-done.2 = bf16[1,544,1024]{2,1,0:T(8,128)(2,1)S(1)} collective-permute-done((bf16[1,544,1024]{2,1,0:T(8,128)(2,1)S(1)}, bf16[1,544,1024]{2,1,0:T(8,128)(2,1)S(1)}, u32[]{:S(2)}, u32[]{:S(2)}) %collective-permute-start.2) | collective-permute-done | bytes 1114144 | tf_op jit(solution)/shard_map/ppermute | solution.py:28
  185.2 22.6 %collective-permute-done.13 = bf16[512,1024]{1,0:T(8,128)(2,1)} collective-permute-done((bf16[512,1024]{1,0:T(8,128)(2,1)S(1)}, bf16[512,1024]{1,0:T(8,128)(2,1)}, u32[]{:S(2)}, u32[]{:S(2)}) %collective-permute-start.13) | collective-permute-done | bytes 1048608 | tf_op jit(solution)/shard_map/ppermute | solution.py:28
  207.8 3.4 collective-permute-start.15
  214.8 2.0 pad_maximum_fusion.2
  216.7 2.0 copy-done
  220.4 10.1 %shard_map.86.refs_0_ = f32[1024,1024]{1,0:T(8,128)S(1)} custom-call(f32[2560,256]{1,0:T(8,128)S(1)} %copy-done.2), custom_call_target="tpu_custom_call" | custom-call | flops 10737418240 | bytes 8388608 | tf_op jit(solution)/shard_map/pallas_call | solution.py:222
  230.6 9.4 %shard_map.87.refs_0_ = f32[1024,1024]{1,0:T(8,128)S(1)} custom-call(f32[1024,1024]{1,0:T(8,128)S(1)} %shard_map.86.refs_0_), custom_call_target="tpu_custom_call" | custom-call | flops 10737418240 | bytes 8388608 | tf_op jit(solution)/shard_map/pallas_call | solution.py:222
  240.0 9.8 %shard_map.88.refs_0_ = f32[1024,1024]{1,0:T(8,128)S(1)} custom-call(f32[1024,1024]{1,0:T(8,128)S(1)} %shard_map.87.refs_0_), custom_call_target="tpu_custom_call" | custom-call | flops 10737418240 | bytes 8388608 | tf_op jit(solution)/shard_map/pallas_call | solution.py:222
  249.8 9.4 %shard_map.89.refs_0_ = f32[1024,1024]{1,0:T(8,128)S(1)} custom-call(f32[1024,1024]{1,0:T(8,128)S(1)} %shard_map.88.refs_0_), custom_call_target="tpu_custom_call" | custom-call | flops 10737418240 | bytes 8388608 | tf_op jit(solution)/shard_map/pallas_call | solution.py:222
  259.2 9.6 %shard_map.90.refs_0_ = f32[1024,1024]{1,0:T(8,128)S(1)} custom-call(f32[1024,1024]{1,0:T(8,128)S(1)} %shard_map.89.refs_0_), custom_call_target="tpu_custom_call" | custom-call | flops 10737418240 | bytes 8388608 | tf_op jit(solution)/shard_map/pallas_call | solution.py:222
  268.8 9.4 %shard_map.91.refs_0_ = f32[1024,1024]{1,0:T(8,128)S(1)} custom-call(f32[1024,1024]{1,0:T(8,128)S(1)} %shard_map.90.refs_0_), custom_call_target="tpu_custom_call" | custom-call | flops 10737418240 | bytes 8388608 | tf_op jit(solution)/shard_map/pallas_call | solution.py:222
  278.1 9.4 %shard_map.92.refs_0_ = f32[1024,1024]{1,0:T(8,128)S(1)} custom-call(f32[1024,1024]{1,0:T(8,128)S(1)} %shard_map.91.refs_0_), custom_call_target="tpu_custom_call" | custom-call | flops 10737418240 | bytes 8388608 | tf_op jit(solution)/shard_map/pallas_call | solution.py:222
  287.5 2.0 copy-done.4
  289.6 4.4 %all-to-all-start = ((bf16[8,128,128]{2,1,0:T(8,128)(2,1)}), bf16[8,128,128]{2,1,0:T(8,128)(2,1)S(1)}, u32[]{:S(2)}, u32[]{:S(2)}) async-start(bf16[8,128,128]{2,1,0:T(8,128)(2,1)} %get-tuple-element.16), calls=%async_computation | async-start | bytes 524288 | tf_op jit(solution)/shard_map/all_to_all | solution.py:366
  293.9 2.2 copy-done.5
  296.1 10.3 %shard_map.93 = (bf16[1024,1024]{1,0:T(8,128)(2,1)S(1)}, bf16[1024,1024]{1,0:T(8,128)(2,1)S(1)}) custom-call(f32[1024,1024]{1,0:T(8,128)S(1)} %copy-done.5), custom_call_target="tpu_custom_call" | custom-call | flops 10737418240 | bytes 8388608 | tf_op jit(solution)/shard_map/pallas_call | solution.py:222
  309.5 2.1 collective-permute-start.18
  311.6 2.3 constant_dynamic-update-slice_fusion.13
  313.9 2.3 constant_dynamic-update-slice_fusion.12
  316.1 2.3 constant_dynamic-update-slice_fusion.11
  318.4 1.9 select_bitcast_fusion.1
  321.7 3.4 convolution_convert_fusion.mixed_ref
  325.2 3.2 collective-permute-done.18
  328.5 4.2 %shard_map.94 = (f32[128,4096]{1,0:T(8,128)}, bf16[128,4096]{1,0:T(8,128)(2,1)S(1)}) custom-call(f32[128,4096]{1,0:T(8,128)S(1)} %copy-done.3, bf16[128,1024]{1,0:T(8,128)(2,1)S(1)} %convolution_convert_fusion.mixed_ref, bf16[4096,1024]{1,0:T(8,128)(2,1)S(1)} %constant_dynamic-update-slice_fusion.10.panel_ref), custom_call_target="tpu_custom_call" | custom-call | flops 1073741824 | bytes 8388608 | tf_op jit(solution)/shard_map/pallas_call | solution.py:285
  332.7 5.7 %convolution_subtract_fusion = f32[1024,128]{1,0:T(8,128)S(1)} fusion(f32[1024,128]{1,0:T(8,128)S(1)} %bitcast.67, bf16[1024,4096]{1,0:T(8,128)(2,1)} %constant_dynamic-update-slice_fusion.2, bf16[128,4096]{1,0:T(8,128)(2,1)S(1)} %get-tuple-element.15), kind=kOutput, calls=%fused_computation.21 | convolution fusion | flops 1073872896 | bytes 10485760 | tf_op jit(solution)/shard_map/dot_general | solution.py:267
  338.5 12.7 %select_convert_fusion.mixed_ref = bf16[2048,1024]{1,0:T(8,128)(2,1)} fusion(s32[2048]{0:T(1024)S(1)} %iota_subtract_fusion, pred[2048]{0:T(1024)(128)(4,1)S(1)} %compare_and_fusion, bf16[2048,1024]{1,0:T(8,128)(2,1)} %constant_dynamic-update-slice_fusion, bf16[2048,1024]{1,0:T(8,128)(2,1)S(1)} %bitcast.65), kind=kOutput, calls=%fused_computation.4 | convolution fusion | flops 8615100416 | bytes 12593152 | tf_op jit(solution)/shard_map/dot_general | solution.py:271
  351.2 13.5 %collective-permute-start.27 = (f32[1024,128]{1,0:T(8,128)S(1)}, f32[1024,128]{1,0:T(8,128)S(1)}, u32[]{:S(2)}, u32[]{:S(2)}) collective-permute-start(f32[1024,128]{1,0:T(8,128)S(1)} %add.233), channel_id=1, source_target_pairs={{0,2},{1,3},{2,0},{3,1},{4,6},{5,7},{6,4},{7,5},{8,10},{9,11},{10,... | collective-permute-start | bytes 1572872 | tf_op jit(solution)/shard_map/ppermute | solution.py:28
  364.8 19.2 %shard_map.95.refs_0_ = f32[2048,4096]{1,0:T(8,128)} custom-call(f32[2048,4096]{1,0:T(8,128)} %inverse_ref.5, bf16[2048,1024]{1,0:T(8,128)(2,1)} %select_convert_fusion.mixed_ref, bf16[4096,1024]{1,0:T(8,128)(2,1)} %copy-done.1), custom_call_target="tpu_custom_call" | custom-call | flops 8589934592 | bytes 33554432 | tf_op jit(solution)/shard_map/pallas_call | solution.py:314
  384.8 5.9 %all-to-all-start.1 = ((f32[8,128,128]{2,1,0:T(8,128)}), f32[8,128,128]{2,1,0:T(8,128)S(1)}, u32[]{:S(2)}, u32[]{:S(2)}) async-start(f32[8,128,128]{2,1,0:T(8,128)} %bitcast.25), calls=%async_computation.1 | async-start | bytes 1048576 | tf_op jit(solution)/shard_map/all_to_all | solution.py:392
  390.7 6.2 %convolution_multiply_fusion = f32[128,4096]{1,0:T(8,128)} fusion(bf16[1024,4096]{1,0:T(8,128)(2,1)} %constant_dynamic-update-slice_fusion.2, f32[1024,128]{1,0:T(8,128)} %add.234), kind=kOutput, calls=%fused_computation.7 | convolution fusion | flops 1074397184 | bytes 11010048 | tf_op jit(solution)/shard_map/dot_general | solution.py:388
  396.9 19.1 %shard_map.96 = f32[2048,4096]{1,0:T(8,128)} custom-call(f32[2048,4096]{1,0:T(8,128)} %inverse_ref.5, bf16[2048,1024]{1,0:T(8,128)(2,1)} %select_convert_fusion.mixed_ref, bf16[4096,1024]{1,0:T(8,128)(2,1)} %copy-done.1, f32[2048,4096]{1,0:T(8,128)} %shard_map.95.refs_0_), custom_call_target="tpu_custom_call", output_to_operand_aliasing={{}: (3, {})} | custom-call | flops 8589934592 | bytes 33554432 | tf_op jit(solution)/shard_map/pallas_call | solution.py:314
  (118 shorter events, 43.9 us)
Async XLA Ops:
  0.6 51.9 %collective-permute-start.19 = (bf16[128,4096]{1,0:T(8,128)(2,1)}, bf16[128,4096]{1,0:T(8,128)(2,1)}, u32[]{:S(2)}, u32[]{:S(2)}) collective-permute-start(bf16[128,4096]{1,0:T(8,128)(2,1)} %param.8), channel_id=1, source_target_pairs={{0,16},{4,20},{8,24},{12,28},{16,0},{20,4},{24,8},{28,12},{1,17},{... | collective-permute-start | bytes 3145736 | tf_op jit(solution)/shard_map/ppermute | solution.py:28
  4.7 46.2 %collective-permute-start.20 = (bf16[128,4096]{1,0:T(8,128)(2,1)}, bf16[128,4096]{1,0:T(8,128)(2,1)}, u32[]{:S(2)}, u32[]{:S(2)}) collective-permute-start(bf16[128,4096]{1,0:T(8,128)(2,1)} %param.8), channel_id=1, source_target_pairs={{0,8},{4,12},{8,0},{12,4},{16,24},{20,28},{24,16},{28,20},{1,9},{5... | collective-permute-start | bytes 3145736 | tf_op jit(solution)/shard_map/ppermute | solution.py:28
  6.3 84.0 %collective-permute-start.21 = (bf16[128,4096]{1,0:T(8,128)(2,1)}, bf16[128,4096]{1,0:T(8,128)(2,1)}, u32[]{:S(2)}, u32[]{:S(2)}) collective-permute-start(bf16[128,4096]{1,0:T(8,128)(2,1)} %param.8), channel_id=1, source_target_pairs={{0,4},{4,0},{8,12},{12,8},{16,20},{20,16},{24,28},{28,24},{1,5},{5... | collective-permute-start | bytes 3145736 | tf_op jit(solution)/shard_map/ppermute | solution.py:28
  14.9 16.1 %collective-permute-start.4 = (f32[2,640,256]{2,1,0:T(8,128)S(1)}, f32[2,640,256]{2,1,0:T(8,128)}, u32[]{:S(2)}, u32[]{:S(2)}) collective-permute-start(f32[2,640,256]{2,1,0:T(8,128)S(1)} %slice_select_fusion), channel_id=1, source_target_pairs={{0,1},{1,0},{2,3},{3,2},{4,5},{5,4},{6,7},{7,6},{8,9},{9,8},{10,11... | collective-permute-start | bytes 3932168 | tf_op jit(solution)/shard_map/ppermute | solution.py:28
  15.0 5.4 %copy-start.3 = (f32[128,4096]{1,0:T(8,128)S(1)}, f32[128,4096]{1,0:T(8,128)}, u32[]{:S(2)}) copy-start(f32[128,4096]{1,0:T(8,128)} %weight_ref.1) | copy-start | bytes 6291460
  21.0 2.1 copy-start.6
  24.8 34.9 %collective-permute-start = (bf16[2,544,1024]{2,1,0:T(8,128)(2,1)}, bf16[2,544,1024]{2,1,0:T(8,128)(2,1)}, u32[]{:S(2)}, u32[]{:S(2)}) collective-permute-start(bf16[2,544,1024]{2,1,0:T(8,128)(2,1)} %broadcast_select_fusion), channel_id=1, source_target_pairs={{0,1},{1,0},{2,3},{3,2},{4,5},{5,4},{6,7},{7,6},{8,9},{9,8},{10,11... | collective-permute-start | bytes 6684680 | tf_op jit(solution)/shard_map/ppermute | solution.py:28
  25.2 4.4 %copy-start.9 = (bf16[128,4096]{1,0:T(8,128)(2,1)S(1)}, bf16[128,4096]{1,0:T(8,128)(2,1)}, u32[]{:S(2)}) copy-start(bf16[128,4096]{1,0:T(8,128)(2,1)} %param.8) | copy-start | bytes 3145732
  25.2 5.5 %copy-start.10 = (bf16[128,256]{1,0:T(8,128)(2,1)S(1)}, bf16[128,256]{1,0:T(8,128)(2,1)}, u32[]{:S(2)}) copy-start(bf16[128,256]{1,0:T(8,128)(2,1)} %param.9) | copy-start | bytes 196612
  31.1 30.0 %slice-start.2 = ((s8[4456448]{0:T(1024)(128)(4,1)}), s8[4194304]{0:T(1024)(128)(4,1)S(1)}, s32[]{:S(2)}) async-start(s8[4456448]{0:T(1024)(128)(4,1)} %bitcast.58), calls=%async_computation.4 | async-start | bytes 8388608
  33.2 27.9 %slice-start.3 = ((s8[4456448]{0:T(1024)(128)(4,1)}), s8[262144]{0:T(1024)(128)(4,1)S(1)}, s32[]{:S(2)}) async-start(s8[4456448]{0:T(1024)(128)(4,1)} %bitcast.58), calls=%async_computation.5 | async-start | bytes 524288
  33.3 23.0 %collective-permute-start.5 = (f32[1,640,256]{2,1,0:T(8,128)S(1)}, f32[1,640,256]{2,1,0:T(8,128)S(1)}, u32[]{:S(2)}, u32[]{:S(2)}) collective-permute-start(f32[1,640,256]{2,1,0:T(8,128)S(1)} %slice_select_fusion.1), channel_id=1, source_target_pairs={{0,2},{1,3},{2,0},{3,1},{4,6},{5,7},{6,4},{7,5},{8,10},{9,11},{10,... | collective-permute-start | bytes 1966088 | tf_op jit(solution)/shard_map/ppermute | solution.py:28
  51.0 64.5 %collective-permute-start.22 = (bf16[128,4096]{1,0:T(8,128)(2,1)}, bf16[128,4096]{1,0:T(8,128)(2,1)S(1)}, u32[]{:S(2)}, u32[]{:S(2)}) collective-permute-start(bf16[128,4096]{1,0:T(8,128)(2,1)} %collective-permute-done.20), channel_id=1, source_target_pairs={{0,4},{4,0},{8,12},{12,8},{16,20},{20,16},{24,28},{28,24},{1,5},{5... | collective-permute-start | bytes 3145736 | tf_op jit(solution)/shard_map/ppermute | solution.py:28
  52.5 41.7 %collective-permute-start.23 = (bf16[128,4096]{1,0:T(8,128)(2,1)}, bf16[128,4096]{1,0:T(8,128)(2,1)S(1)}, u32[]{:S(2)}, u32[]{:S(2)}) collective-permute-start(bf16[128,4096]{1,0:T(8,128)(2,1)} %collective-permute-done.19), channel_id=1, source_target_pairs={{0,8},{4,12},{8,0},{12,4},{16,24},{20,28},{24,16},{28,20},{1,9},{5... | collective-permute-start | bytes 3145736 | tf_op jit(solution)/shard_map/ppermute | solution.py:28
  56.4 33.0 %collective-permute-start.6 = (f32[1,640,256]{2,1,0:T(8,128)S(1)}, f32[1,640,256]{2,1,0:T(8,128)S(1)}, u32[]{:S(2)}, u32[]{:S(2)}) collective-permute-start(f32[1,640,256]{2,1,0:T(8,128)S(1)} %select_select_fusion.3), channel_id=1, source_target_pairs={{0,16},{4,20},{8,24},{12,28},{16,0},{20,4},{24,8},{28,12},{1,17},{... | collective-permute-start | bytes 1966088 | tf_op jit(solution)/shard_map/ppermute | solution.py:28
  59.7 86.2 %collective-permute-start.24 = (bf16[128,4096]{1,0:T(8,128)(2,1)}, bf16[128,4096]{1,0:T(8,128)(2,1)S(1)}, u32[]{:S(2)}, u32[]{:S(2)}) collective-permute-start(bf16[128,4096]{1,0:T(8,128)(2,1)} %collective-permute-done.19), channel_id=1, source_target_pairs={{0,4},{4,0},{8,12},{12,8},{16,20},{20,16},{24,28},{28,24},{1,5},{5... | collective-permute-start | bytes 3145736 | tf_op jit(solution)/shard_map/ppermute | solution.py:28
  89.6 24.2 %collective-permute-start.7 = (f32[1,640,256]{2,1,0:T(8,128)S(1)}, f32[1,640,256]{2,1,0:T(8,128)S(1)}, u32[]{:S(2)}, u32[]{:S(2)}) collective-permute-start(f32[1,640,256]{2,1,0:T(8,128)S(1)} %broadcast_select_fusion.2), channel_id=1, source_target_pairs={{0,4},{4,0},{8,12},{12,8},{16,20},{20,16},{24,28},{28,24},{1,5},{5... | collective-permute-start | bytes 1966088 | tf_op jit(solution)/shard_map/ppermute | solution.py:28
  90.3 26.2 %collective-permute-start.1 = (bf16[1,544,1024]{2,1,0:T(8,128)(2,1)S(1)}, bf16[1,544,1024]{2,1,0:T(8,128)(2,1)S(1)}, u32[]{:S(2)}, u32[]{:S(2)}) collective-permute-start(bf16[1,544,1024]{2,1,0:T(8,128)(2,1)S(1)} %broadcast_select_fusion.1), channel_id=1, source_target_pairs={{0,2},{1,3},{2,0},{3,1},{4,6},{5,7},{6,4},{7,5},{8,10},{9,11},{10,... | collective-permute-start | bytes 3342344 | tf_op jit(solution)/shard_map/ppermute | solution.py:28
  94.2 78.0 %collective-permute-start.25 = (bf16[128,4096]{1,0:T(8,128)(2,1)S(1)}, bf16[128,4096]{1,0:T(8,128)(2,1)S(1)}, u32[]{:S(2)}, u32[]{:S(2)}) collective-permute-start(bf16[128,4096]{1,0:T(8,128)(2,1)S(1)} %collective-permute-done.23), channel_id=1, source_target_pairs={{0,4},{4,0},{8,12},{12,8},{16,20},{20,16},{24,28},{28,24},{1,5},{5... | collective-permute-start | bytes 3145736 | tf_op jit(solution)/shard_map/ppermute | solution.py:28
  113.9 28.8 %collective-permute-start.8 = (f32[1,640,256]{2,1,0:T(8,128)S(1)}, f32[1,640,256]{2,1,0:T(8,128)S(1)}, u32[]{:S(2)}, u32[]{:S(2)}) collective-permute-start(f32[1,640,256]{2,1,0:T(8,128)S(1)} %broadcast_select_fusion.3), channel_id=1, source_target_pairs={{0,8},{4,12},{8,0},{12,4},{16,24},{20,28},{24,16},{28,20},{1,9},{5... | collective-permute-start | bytes 1966088 | tf_op jit(solution)/shard_map/ppermute | solution.py:28
  116.7 30.2 %collective-permute-start.11 = (bf16[512,1024]{1,0:T(8,128)(2,1)S(1)}, bf16[512,1024]{1,0:T(8,128)(2,1)S(1)}, u32[]{:S(2)}, u32[]{:S(2)}) collective-permute-start(bf16[512,1024]{1,0:T(8,128)(2,1)S(1)} %slice_bitcast_fusion), channel_id=1, source_target_pairs={{0,0},{4,4},{2,8},{6,12},{1,16},{5,20},{3,24},{7,28},{8,1},{12,5},... | collective-permute-start | bytes 3145736 | tf_op jit(solution)/shard_map/ppermute | solution.py:63
  142.7 27.5 %collective-permute-start.9 = (f32[1,640,256]{2,1,0:T(8,128)S(1)}, f32[1,640,256]{2,1,0:T(8,128)S(1)}, u32[]{:S(2)}, u32[]{:S(2)}) collective-permute-start(f32[1,640,256]{2,1,0:T(8,128)S(1)} %broadcast_select_fusion.4), channel_id=1, source_target_pairs={{0,2},{1,3},{2,0},{3,1},{4,6},{5,7},{6,4},{7,5},{8,10},{9,11},{10,... | collective-permute-start | bytes 1966088 | tf_op jit(solution)/shard_map/ppermute | solution.py:28
  143.9 39.4 %collective-permute-start.2 = (bf16[1,544,1024]{2,1,0:T(8,128)(2,1)S(1)}, bf16[1,544,1024]{2,1,0:T(8,128)(2,1)S(1)}, u32[]{:S(2)}, u32[]{:S(2)}) collective-permute-start(bf16[1,544,1024]{2,1,0:T(8,128)(2,1)S(1)} %select_select_fusion.2), channel_id=1, source_target_pairs={{0,2},{1,3},{2,0},{3,1},{4,6},{5,7},{6,4},{7,5},{8,10},{9,11},{10,... | collective-permute-start | bytes 3342344 | tf_op jit(solution)/shard_map/ppermute | solution.py:28
  146.9 64.3 %collective-permute-start.12 = (bf16[512,1024]{1,0:T(8,128)(2,1)S(1)}, bf16[512,1024]{1,0:T(8,128)(2,1)}, u32[]{:S(2)}, u32[]{:S(2)}) collective-permute-start(bf16[512,1024]{1,0:T(8,128)(2,1)S(1)} %collective-permute-done.11), channel_id=1, source_target_pairs={{0,16},{4,20},{8,24},{12,28},{16,0},{20,4},{24,8},{28,12},{1,17},{... | collective-permute-start | bytes 3145736 | tf_op jit(solution)/shard_map/ppermute | solution.py:28
  167.7 40.1 %collective-permute-start.13 = (bf16[512,1024]{1,0:T(8,128)(2,1)S(1)}, bf16[512,1024]{1,0:T(8,128)(2,1)}, u32[]{:S(2)}, u32[]{:S(2)}) collective-permute-start(bf16[512,1024]{1,0:T(8,128)(2,1)S(1)} %collective-permute-done.11), channel_id=1, source_target_pairs={{0,8},{4,12},{8,0},{12,4},{16,24},{20,28},{24,16},{28,20},{1,9},{5... | collective-permute-start | bytes 3145736 | tf_op jit(solution)/shard_map/ppermute | solution.py:28
  170.2 44.1 %collective-permute-start.14 = (bf16[512,1024]{1,0:T(8,128)(2,1)S(1)}, bf16[512,1024]{1,0:T(8,128)(2,1)S(1)}, u32[]{:S(2)}, u32[]{:S(2)}) collective-permute-start(bf16[512,1024]{1,0:T(8,128)(2,1)S(1)} %collective-permute-done.11), channel_id=1, source_target_pairs={{0,4},{4,0},{8,12},{12,8},{16,20},{20,16},{24,28},{28,24},{1,5},{5... | collective-permute-start | bytes 3145736 | tf_op jit(solution)/shard_map/ppermute | solution.py:28
  172.2 42.3 %collective-permute-start.10 = (f32[2,640,256]{2,1,0:T(8,128)S(1)}, f32[2,640,256]{2,1,0:T(8,128)S(1)}, u32[]{:S(2)}, u32[]{:S(2)}) collective-permute-start(f32[2,640,256]{2,1,0:T(8,128)S(1)} %maximum_bitcast_fusion.1), channel_id=1, source_target_pairs={{0,1},{1,0},{2,3},{3,2},{4,5},{5,4},{6,7},{7,6},{8,9},{9,8},{10,11... | collective-permute-start | bytes 3932168 | tf_op jit(solution)/shard_map/ppermute | solution.py:28
  183.5 30.8 %copy-start.7 = (bf16[1,1,544,1024]{3,2,1,0:T(8,128)(2,1)}, bf16[1,1,544,1024]{3,2,1,0:T(8,128)(2,1)S(1)}, u32[]{:S(2)}) copy-start(bf16[1,1,544,1024]{3,2,1,0:T(8,128)(2,1)S(1)} %get-tuple-element.25) | copy-start | bytes 3342340
  185.2 133.2 %collective-permute-start.3 = (bf16[2,544,1024]{2,1,0:T(8,128)(2,1)}, bf16[2,544,1024]{2,1,0:T(8,128)(2,1)}, u32[]{:S(2)}, u32[]{:S(2)}) collective-permute-start(bf16[2,544,1024]{2,1,0:T(8,128)(2,1)} %maximum_bitcast_fusion), channel_id=1, source_target_pairs={{0,1},{1,0},{2,3},{3,2},{4,5},{5,4},{6,7},{7,6},{8,9},{9,8},{10,11... | collective-permute-start | bytes 6684680 | tf_op jit(solution)/shard_map/ppermute | solution.py:28
  207.8 103.8 %collective-permute-start.15 = (bf16[512,1024]{1,0:T(8,128)(2,1)}, bf16[512,1024]{1,0:T(8,128)(2,1)}, u32[]{:S(2)}, u32[]{:S(2)}) collective-permute-start(bf16[512,1024]{1,0:T(8,128)(2,1)} %collective-permute-done.13), channel_id=1, source_target_pairs={{0,4},{4,0},{8,12},{12,8},{16,20},{20,16},{24,28},{28,24},{1,5},{5... | collective-permute-start | bytes 3145736 | tf_op jit(solution)/shard_map/ppermute | solution.py:28
  211.2 98.3 %collective-permute-start.16 = (bf16[512,1024]{1,0:T(8,128)(2,1)}, bf16[512,1024]{1,0:T(8,128)(2,1)}, u32[]{:S(2)}, u32[]{:S(2)}) collective-permute-start(bf16[512,1024]{1,0:T(8,128)(2,1)} %collective-permute-done.12), channel_id=1, source_target_pairs={{0,8},{4,12},{8,0},{12,4},{16,24},{20,28},{24,16},{28,20},{1,9},{5... | collective-permute-start | bytes 3145736 | tf_op jit(solution)/shard_map/ppermute | solution.py:28
  214.3 101.8 %collective-permute-start.17 = (bf16[512,1024]{1,0:T(8,128)(2,1)}, bf16[512,1024]{1,0:T(8,128)(2,1)}, u32[]{:S(2)}, u32[]{:S(2)}) collective-permute-start(bf16[512,1024]{1,0:T(8,128)(2,1)} %collective-permute-done.12), channel_id=1, source_target_pairs={{0,4},{4,0},{8,12},{12,8},{16,20},{20,16},{24,28},{28,24},{1,5},{5... | collective-permute-start | bytes 3145736 | tf_op jit(solution)/shard_map/ppermute | solution.py:28
  214.5 4.2 %copy-start = (bf16[4096,1024]{1,0:T(8,128)(2,1)}, bf16[4096,1024]{1,0:T(8,128)(2,1)S(1)}, u32[]{:S(2)}) copy-start(bf16[4096,1024]{1,0:T(8,128)(2,1)S(1)} %constant_dynamic-update-slice_fusion.14) | copy-start | bytes 25165828
  218.7 1.7 copy-start.2
  287.5 2.0 copy-start.4
  289.6 19.9 %all-to-all-start = ((bf16[8,128,128]{2,1,0:T(8,128)(2,1)}), bf16[8,128,128]{2,1,0:T(8,128)(2,1)S(1)}, u32[]{:S(2)}, u32[]{:S(2)}) async-start(bf16[8,128,128]{2,1,0:T(8,128)(2,1)} %get-tuple-element.16), calls=%async_computation | async-start | bytes 524288 | tf_op jit(solution)/shard_map/all_to_all | solution.py:366
  293.9 2.2 copy-start.5
  309.5 8.9 %copy-start.8 = (bf16[1,1,544,1024]{3,2,1,0:T(8,128)(2,1)S(1)}, bf16[1,1,544,1024]{3,2,1,0:T(8,128)(2,1)}, u32[]{:S(2)}) copy-start(bf16[1,1,544,1024]{3,2,1,0:T(8,128)(2,1)} %copy-done.7) | copy-start | bytes 3342340
  309.5 18.9 %collective-permute-start.18 = (bf16[512,1024]{1,0:T(8,128)(2,1)}, bf16[512,1024]{1,0:T(8,128)(2,1)S(1)}, u32[]{:S(2)}, u32[]{:S(2)}) collective-permute-start(bf16[512,1024]{1,0:T(8,128)(2,1)} %collective-permute-done.16), channel_id=1, source_target_pairs={{0,4},{4,0},{8,12},{12,8},{16,20},{20,16},{24,28},{28,24},{1,5},{5... | collective-permute-start | bytes 3145736 | tf_op jit(solution)/shard_map/ppermute | solution.py:28
  320.7 7.6 %slice-start = ((s8[8388608]{0:T(1024)(128)(4,1)}), s8[4194304]{0:T(1024)(128)(4,1)S(1)}, s32[]{:S(2)}) async-start(s8[8388608]{0:T(1024)(128)(4,1)} %bitcast.55), calls=%async_computation.2 | async-start | bytes 8388608
  321.2 7.1 %slice-start.1 = ((s8[8388608]{0:T(1024)(128)(4,1)}), s8[4194304]{0:T(1024)(128)(4,1)S(1)}, s32[]{:S(2)}) async-start(s8[8388608]{0:T(1024)(128)(4,1)} %bitcast.55), calls=%async_computation.3 | async-start | bytes 8388608
  328.5 4.2 %copy-start.1 = (bf16[4096,1024]{1,0:T(8,128)(2,1)}, bf16[4096,1024]{1,0:T(8,128)(2,1)S(1)}, u32[]{:S(2)}) copy-start(bf16[4096,1024]{1,0:T(8,128)(2,1)S(1)} %constant_dynamic-update-slice_fusion.10.panel_ref) | copy-start | bytes 25165828
  338.4 12.8 %collective-permute-start.26 = (f32[1024,128]{1,0:T(8,128)S(1)}, f32[1024,128]{1,0:T(8,128)S(1)}, u32[]{:S(2)}, u32[]{:S(2)}) collective-permute-start(f32[1024,128]{1,0:T(8,128)S(1)} %convolution_subtract_fusion), channel_id=1, source_target_pairs={{0,1},{1,0},{2,3},{3,2},{4,5},{5,4},{6,7},{7,6},{8,9},{9,8},{10,11... | collective-permute-start | bytes 1572872 | tf_op jit(solution)/shard_map/ppermute | solution.py:28
  351.2 32.7 %collective-permute-start.27 = (f32[1024,128]{1,0:T(8,128)S(1)}, f32[1024,128]{1,0:T(8,128)S(1)}, u32[]{:S(2)}, u32[]{:S(2)}) collective-permute-start(f32[1024,128]{1,0:T(8,128)S(1)} %add.233), channel_id=1, source_target_pairs={{0,2},{1,3},{2,0},{3,1},{4,6},{5,7},{6,4},{7,5},{8,10},{9,11},{10,... | collective-permute-start | bytes 1572872 | tf_op jit(solution)/shard_map/ppermute | solution.py:28
  384.8 31.2 %all-to-all-start.1 = ((f32[8,128,128]{2,1,0:T(8,128)}), f32[8,128,128]{2,1,0:T(8,128)S(1)}, u32[]{:S(2)}, u32[]{:S(2)}) async-start(f32[8,128,128]{2,1,0:T(8,128)} %bitcast.25), calls=%async_computation.1 | async-start | bytes 1048576 | tf_op jit(solution)/shard_map/all_to_all | solution.py:392

commit v3 on v2

--- a/solution.py
+++ b/solution.py
@@ -107,11 +107,19 @@
     return out
 
 
-def dot32(a, b):
-    ah, bh = a.astype(BF16), b.astype(BF16)
-    al, bl = (a - ah.astype(F32)).astype(BF16), (b - bh.astype(F32)).astype(BF16)
-    dot = functools.partial(jnp.dot, preferred_element_type=F32)
-    return dot(ah, bh) + (dot(ah, bl) + dot(al, bh))
+def terms(x):
+    high = x.astype(BF16)
+    return high, (x - high.astype(F32)).astype(BF16)
+
+
+def left_terms(a):
+    high, low = terms(a)
+    return jnp.concatenate([high, low, high], 1)
+
+
+def right_terms(b):
+    high, low = terms(b)
+    return jnp.concatenate([high, high, low], 0)
 
 
 def wide(x, n):
@@ -184,13 +192,14 @@
         ]
         pivot = jnp.concatenate(sweep(t), 0)
         a_ref[pl.ds(o, NB), pl.ds(o, NB)] = eye
-        new = dot32(pivot, a_ref[pl.ds(o, NB), :])
+        new = nn(left_terms(pivot), right_terms(a_ref[pl.ds(o, NB), :]))
+        right = right_terms(new)
 
         def update(i, _):
             r = pl.multiple_of(i * TILE, TILE)
             c = a_ref[pl.ds(r, TILE), pl.ds(o, NB)]
             a_ref[pl.ds(r, TILE), pl.ds(o, NB)] = jnp.zeros((TILE, NB), F32)
-            a_ref[pl.ds(r, TILE), :] = a_ref[pl.ds(r, TILE), :] - dot32(c, new)
+            a_ref[pl.ds(r, TILE), :] = a_ref[pl.ds(r, TILE), :] - nn(left_terms(c), right)
             return 0
 
         lax.fori_loop(0, n // TILE, update, 0)

time: 423 us -> 419 us (level)
  Pallas kernels: 124 us -> 119 us
    pallas_call x8, Pallas kernels: 77.3 us -> 72.9 us  [inverse_call(): pl.pallas_call(functools.partial(inverse_kernel, first, GROUPS), out_shap...]
  transfers between devices with their start and end apart: 30 -> 30, of which waited for: 7 -> 7; matrix products, arithmetic and copies ran while one was open for 18% -> 18% of each run, Pallas kernels for 29% -> 28%
where the time goes in v3:
time: 419 us; the launch traced here: 413 us
  waiting for transfers between devices  121 us (29%)
  Pallas kernels  119 us (28%)
  starting transfers between devices  77.8 us (19%)
  local copies, waits for them, and re-layouts  47 us (11%)
  matrix products  28 us (7%)
  other arithmetic  16.9 us (4%)
    ppermute x27, waiting for transfers between devices, swap(): return lax.ppermute(x, axis, [(i, i ^ bit) for i in range(n)])  121 us
    pallas_call x8, Pallas kernels, inverse_call(): pl.pallas_call(functools.partial(inverse_kernel, first, GROUPS), out_shap...  72.9 us
    ppermute x27, starting transfers between devices, swap(): return lax.ppermute(x, axis, [(i, i ^ bit) for i in range(n)])  66.6 us
    pallas_call x2, Pallas kernels, remove_from_inverse(): pl.pallas_call(inverse_step_kernel, grid=(count,), out_shape=jax.ShapeDty...  38.3 us
    dynamic_update_slice x16, local copies, waits for them, and re-layouts, assemble(): lax.dynamic_update_slice_in_dim(out, part, start(lax.axis_index('row') ^...  22.1 us
    dot_general x2, matrix products, nn(): lax.dot_general(a, b, (((1,), (0,)), ((), ())), preferred_element_type=F32)  16.1 us
    unnamed x32, local copies, waits for them, and re-layouts  11.7 us
  transfers between devices with their start and end apart: 30, of which 7 were waited for; matrix products, arithmetic and copies ran while one was open for 18% of the time, Pallas kernels for 28%

profile of v3, /device:TPU:0, one launch (start us, length us, event | category | flops | bytes accessed | tf_op | source)
XLA Modules:
  0.0 412.7 jit_solution(12608237315304713998)
XLA Ops:
  0.6 4.1 collective-permute-start.19
  9.1 4.0 shard_map.84
  13.0 1.9 slice_select_fusion
  15.0 5.0 %dynamic-slice_convert_fusion = bf16[2048,1024]{1,0:T(8,128)(2,1)S(1)} fusion(f32[2048,4096]{1,0:T(8,128)} %inverse_ref.5, s32[]{:T(128)S(6)} %select_n.331), kind=kLoop, calls=%fused_computation.5 | loop fusion | bytes 8388612 | tf_op jit(solution)/shard_map/convert_element_type | solution.py:360
  20.7 2.1 copy-done.6
  24.9 4.3 %broadcast_in_dim.11 = bf16[1024,4096]{1,0:T(8,128)(2,1)} broadcast(bf16[]{:T(256)} %constant.263.clone.1), dimensions={} | broadcast | bytes 8388610 | tf_op jit(solution)/shard_map/broadcast_in_dim | solution.py:104
  30.8 2.1 select_select_fusion.1
  35.3 15.6 %collective-permute-done.20 = bf16[128,4096]{1,0:T(8,128)(2,1)} collective-permute-done((bf16[128,4096]{1,0:T(8,128)(2,1)}, bf16[128,4096]{1,0:T(8,128)(2,1)}, u32[]{:S(2)}, u32[]{:S(2)}) %collective-permute-start.20) | collective-permute-done | bytes 1048608 | tf_op jit(solution)/shard_map/ppermute | solution.py:28
  54.0 2.3 constant_dynamic-update-slice_fusion.8
  57.4 2.3 constant_dynamic-update-slice_fusion.7
  61.7 27.8 %collective-permute-done.6 = f32[1,640,256]{2,1,0:T(8,128)S(1)} collective-permute-done((f32[1,640,256]{2,1,0:T(8,128)S(1)}, f32[1,640,256]{2,1,0:T(8,128)S(1)}, u32[]{:S(2)}, u32[]{:S(2)}) %collective-permute-start.6) | collective-permute-done | bytes 655392 | tf_op jit(solution)/shard_map/ppermute | solution.py:28
  91.9 2.3 constant_dynamic-update-slice_fusion.6
  95.7 18.1 %collective-permute-done.7 = f32[1,640,256]{2,1,0:T(8,128)S(1)} collective-permute-done((f32[1,640,256]{2,1,0:T(8,128)S(1)}, f32[1,640,256]{2,1,0:T(8,128)S(1)}, u32[]{:S(2)}, u32[]{:S(2)}) %collective-permute-start.7) | collective-permute-done | bytes 655392 | tf_op jit(solution)/shard_map/ppermute | solution.py:28
  117.7 25.0 %collective-permute-done.8 = f32[1,640,256]{2,1,0:T(8,128)S(1)} collective-permute-done((f32[1,640,256]{2,1,0:T(8,128)S(1)}, f32[1,640,256]{2,1,0:T(8,128)S(1)}, u32[]{:S(2)}, u32[]{:S(2)}) %collective-permute-start.8) | collective-permute-done | bytes 655392 | tf_op jit(solution)/shard_map/ppermute | solution.py:28
  143.9 2.0 collective-permute-start.2
  146.9 20.7 %collective-permute-start.12 = (bf16[512,1024]{1,0:T(8,128)(2,1)S(1)}, bf16[512,1024]{1,0:T(8,128)(2,1)}, u32[]{:S(2)}, u32[]{:S(2)}) collective-permute-start(bf16[512,1024]{1,0:T(8,128)(2,1)S(1)} %collective-permute-done.11), channel_id=1, source_target_pairs={{0,16},{4,20},{8,24},{12,28},{16,0},{20,4},{24,8},{28,12},{1,17},{... | collective-permute-start | bytes 3145736 | tf_op jit(solution)/shard_map/ppermute | solution.py:28
  167.7 2.5 collective-permute-start.13
  174.6 8.7 %collective-permute-done.2 = bf16[1,544,1024]{2,1,0:T(8,128)(2,1)S(1)} collective-permute-done((bf16[1,544,1024]{2,1,0:T(8,128)(2,1)S(1)}, bf16[1,544,1024]{2,1,0:T(8,128)(2,1)S(1)}, u32[]{:S(2)}, u32[]{:S(2)}) %collective-permute-start.2) | collective-permute-done | bytes 1114144 | tf_op jit(solution)/shard_map/ppermute | solution.py:28
  185.2 22.6 %collective-permute-done.13 = bf16[512,1024]{1,0:T(8,128)(2,1)} collective-permute-done((bf16[512,1024]{1,0:T(8,128)(2,1)S(1)}, bf16[512,1024]{1,0:T(8,128)(2,1)}, u32[]{:S(2)}, u32[]{:S(2)}) %collective-permute-start.13) | collective-permute-done | bytes 1048608 | tf_op jit(solution)/shard_map/ppermute | solution.py:28
  207.8 3.4 collective-permute-start.15
  214.8 2.0 pad_maximum_fusion.2
  216.7 2.0 copy-done
  220.4 9.5 %shard_map.86.refs_0_ = f32[1024,1024]{1,0:T(8,128)S(1)} custom-call(f32[2560,256]{1,0:T(8,128)S(1)} %copy-done.2), custom_call_target="tpu_custom_call" | custom-call | flops 10737418240 | bytes 8388608 | tf_op jit(solution)/shard_map/pallas_call | solution.py:231
  230.0 8.9 %shard_map.87.refs_0_ = f32[1024,1024]{1,0:T(8,128)S(1)} custom-call(f32[1024,1024]{1,0:T(8,128)S(1)} %shard_map.86.refs_0_), custom_call_target="tpu_custom_call" | custom-call | flops 10737418240 | bytes 8388608 | tf_op jit(solution)/shard_map/pallas_call | solution.py:231
  238.8 9.3 %shard_map.88.refs_0_ = f32[1024,1024]{1,0:T(8,128)S(1)} custom-call(f32[1024,1024]{1,0:T(8,128)S(1)} %shard_map.87.refs_0_), custom_call_target="tpu_custom_call" | custom-call | flops 10737418240 | bytes 8388608 | tf_op jit(solution)/shard_map/pallas_call | solution.py:231
  248.2 8.9 %shard_map.89.refs_0_ = f32[1024,1024]{1,0:T(8,128)S(1)} custom-call(f32[1024,1024]{1,0:T(8,128)S(1)} %shard_map.88.refs_0_), custom_call_target="tpu_custom_call" | custom-call | flops 10737418240 | bytes 8388608 | tf_op jit(solution)/shard_map/pallas_call | solution.py:231
  257.0 9.0 %shard_map.90.refs_0_ = f32[1024,1024]{1,0:T(8,128)S(1)} custom-call(f32[1024,1024]{1,0:T(8,128)S(1)} %shard_map.89.refs_0_), custom_call_target="tpu_custom_call" | custom-call | flops 10737418240 | bytes 8388608 | tf_op jit(solution)/shard_map/pallas_call | solution.py:231
  266.0 8.8 %shard_map.91.refs_0_ = f32[1024,1024]{1,0:T(8,128)S(1)} custom-call(f32[1024,1024]{1,0:T(8,128)S(1)} %shard_map.90.refs_0_), custom_call_target="tpu_custom_call" | custom-call | flops 10737418240 | bytes 8388608 | tf_op jit(solution)/shard_map/pallas_call | solution.py:231
  274.8 8.8 %shard_map.92.refs_0_ = f32[1024,1024]{1,0:T(8,128)S(1)} custom-call(f32[1024,1024]{1,0:T(8,128)S(1)} %shard_map.91.refs_0_), custom_call_target="tpu_custom_call" | custom-call | flops 10737418240 | bytes 8388608 | tf_op jit(solution)/shard_map/pallas_call | solution.py:231
  283.7 2.0 copy-done.4
  285.7 4.4 %all-to-all-start = ((bf16[8,128,128]{2,1,0:T(8,128)(2,1)}), bf16[8,128,128]{2,1,0:T(8,128)(2,1)S(1)}, u32[]{:S(2)}, u32[]{:S(2)}) async-start(bf16[8,128,128]{2,1,0:T(8,128)(2,1)} %get-tuple-element.16), calls=%async_computation | async-start | bytes 524288 | tf_op jit(solution)/shard_map/all_to_all | solution.py:375
  290.1 2.2 copy-done.5
  292.3 9.8 %shard_map.93 = (bf16[1024,1024]{1,0:T(8,128)(2,1)S(1)}, bf16[1024,1024]{1,0:T(8,128)(2,1)S(1)}) custom-call(f32[1024,1024]{1,0:T(8,128)S(1)} %copy-done.5), custom_call_target="tpu_custom_call" | custom-call | flops 10737418240 | bytes 8388608 | tf_op jit(solution)/shard_map/pallas_call | solution.py:231
  305.1 2.1 collective-permute-start.18
  307.2 2.3 constant_dynamic-update-slice_fusion.13
  309.5 2.3 constant_dynamic-update-slice_fusion.12
  311.7 2.3 constant_dynamic-update-slice_fusion.11
  314.0 1.9 select_bitcast_fusion.1
  317.4 3.4 convolution_convert_fusion.mixed_ref
  320.8 3.2 collective-permute-done.18
  324.1 4.2 %shard_map.94 = (f32[128,4096]{1,0:T(8,128)}, bf16[128,4096]{1,0:T(8,128)(2,1)S(1)}) custom-call(f32[128,4096]{1,0:T(8,128)S(1)} %copy-done.3, bf16[128,1024]{1,0:T(8,128)(2,1)S(1)} %convolution_convert_fusion.mixed_ref, bf16[4096,1024]{1,0:T(8,128)(2,1)S(1)} %constant_dynamic-update-slice_fusion.10.panel_ref), custom_call_target="tpu_custom_call" | custom-call | flops 1073741824 | bytes 8388608 | tf_op jit(solution)/shard_map/pallas_call | solution.py:294
  328.3 5.7 %convolution_subtract_fusion = f32[1024,128]{1,0:T(8,128)S(1)} fusion(f32[1024,128]{1,0:T(8,128)S(1)} %bitcast.67, bf16[1024,4096]{1,0:T(8,128)(2,1)} %constant_dynamic-update-slice_fusion.2, bf16[128,4096]{1,0:T(8,128)(2,1)S(1)} %get-tuple-element.15), kind=kOutput, calls=%fused_computation.21 | convolution fusion | flops 1073872896 | bytes 10485760 | tf_op jit(solution)/shard_map/dot_general | solution.py:276
  334.1 12.7 %select_convert_fusion.mixed_ref = bf16[2048,1024]{1,0:T(8,128)(2,1)} fusion(s32[2048]{0:T(1024)S(1)} %iota_subtract_fusion, pred[2048]{0:T(1024)(128)(4,1)S(1)} %compare_and_fusion, bf16[2048,1024]{1,0:T(8,128)(2,1)} %constant_dynamic-update-slice_fusion, bf16[2048,1024]{1,0:T(8,128)(2,1)S(1)} %bitcast.65), kind=kOutput, calls=%fused_computation.4 | convolution fusion | flops 8615100416 | bytes 12593152 | tf_op jit(solution)/shard_map/dot_general | solution.py:280
  346.9 13.4 %collective-permute-start.27 = (f32[1024,128]{1,0:T(8,128)S(1)}, f32[1024,128]{1,0:T(8,128)S(1)}, u32[]{:S(2)}, u32[]{:S(2)}) collective-permute-start(f32[1024,128]{1,0:T(8,128)S(1)} %add.233), channel_id=1, source_target_pairs={{0,2},{1,3},{2,0},{3,1},{4,6},{5,7},{6,4},{7,5},{8,10},{9,11},{10,... | collective-permute-start | bytes 1572872 | tf_op jit(solution)/shard_map/ppermute | solution.py:28
  360.3 19.2 %shard_map.95.refs_0_ = f32[2048,4096]{1,0:T(8,128)} custom-call(f32[2048,4096]{1,0:T(8,128)} %inverse_ref.5, bf16[2048,1024]{1,0:T(8,128)(2,1)} %select_convert_fusion.mixed_ref, bf16[4096,1024]{1,0:T(8,128)(2,1)} %copy-done.1), custom_call_target="tpu_custom_call" | custom-call | flops 8589934592 | bytes 33554432 | tf_op jit(solution)/shard_map/pallas_call | solution.py:323
  380.4 5.9 %all-to-all-start.1 = ((f32[8,128,128]{2,1,0:T(8,128)}), f32[8,128,128]{2,1,0:T(8,128)S(1)}, u32[]{:S(2)}, u32[]{:S(2)}) async-start(f32[8,128,128]{2,1,0:T(8,128)} %bitcast.25), calls=%async_computation.1 | async-start | bytes 1048576 | tf_op jit(solution)/shard_map/all_to_all | solution.py:401
  386.3 6.2 %convolution_multiply_fusion = f32[128,4096]{1,0:T(8,128)} fusion(bf16[1024,4096]{1,0:T(8,128)(2,1)} %constant_dynamic-update-slice_fusion.2, f32[1024,128]{1,0:T(8,128)} %add.234), kind=kOutput, calls=%fused_computation.7 | convolution fusion | flops 1074397184 | bytes 11010048 | tf_op jit(solution)/shard_map/dot_general | solution.py:397
  392.5 19.1 %shard_map.96 = f32[2048,4096]{1,0:T(8,128)} custom-call(f32[2048,4096]{1,0:T(8,128)} %inverse_ref.5, bf16[2048,1024]{1,0:T(8,128)(2,1)} %select_convert_fusion.mixed_ref, bf16[4096,1024]{1,0:T(8,128)(2,1)} %copy-done.1, f32[2048,4096]{1,0:T(8,128)} %shard_map.95.refs_0_), custom_call_target="tpu_custom_call", output_to_operand_aliasing={{}: (3, {})} | custom-call | flops 8589934592 | bytes 33554432 | tf_op jit(solution)/shard_map/pallas_call | solution.py:323
  (118 shorter events, 43.9 us)
Async XLA Ops:
  0.6 51.9 %collective-permute-start.19 = (bf16[128,4096]{1,0:T(8,128)(2,1)}, bf16[128,4096]{1,0:T(8,128)(2,1)}, u32[]{:S(2)}, u32[]{:S(2)}) collective-permute-start(bf16[128,4096]{1,0:T(8,128)(2,1)} %param.8), channel_id=1, source_target_pairs={{0,16},{4,20},{8,24},{12,28},{16,0},{20,4},{24,8},{28,12},{1,17},{... | collective-permute-start | bytes 3145736 | tf_op jit(solution)/shard_map/ppermute | solution.py:28
  4.7 46.2 %collective-permute-start.20 = (bf16[128,4096]{1,0:T(8,128)(2,1)}, bf16[128,4096]{1,0:T(8,128)(2,1)}, u32[]{:S(2)}, u32[]{:S(2)}) collective-permute-start(bf16[128,4096]{1,0:T(8,128)(2,1)} %param.8), channel_id=1, source_target_pairs={{0,8},{4,12},{8,0},{12,4},{16,24},{20,28},{24,16},{28,20},{1,9},{5... | collective-permute-start | bytes 3145736 | tf_op jit(solution)/shard_map/ppermute | solution.py:28
  6.3 84.0 %collective-permute-start.21 = (bf16[128,4096]{1,0:T(8,128)(2,1)}, bf16[128,4096]{1,0:T(8,128)(2,1)}, u32[]{:S(2)}, u32[]{:S(2)}) collective-permute-start(bf16[128,4096]{1,0:T(8,128)(2,1)} %param.8), channel_id=1, source_target_pairs={{0,4},{4,0},{8,12},{12,8},{16,20},{20,16},{24,28},{28,24},{1,5},{5... | collective-permute-start | bytes 3145736 | tf_op jit(solution)/shard_map/ppermute | solution.py:28
  14.9 15.8 %collective-permute-start.4 = (f32[2,640,256]{2,1,0:T(8,128)S(1)}, f32[2,640,256]{2,1,0:T(8,128)}, u32[]{:S(2)}, u32[]{:S(2)}) collective-permute-start(f32[2,640,256]{2,1,0:T(8,128)S(1)} %slice_select_fusion), channel_id=1, source_target_pairs={{0,1},{1,0},{2,3},{3,2},{4,5},{5,4},{6,7},{7,6},{8,9},{9,8},{10,11... | collective-permute-start | bytes 3932168 | tf_op jit(solution)/shard_map/ppermute | solution.py:28
  15.0 5.1 %copy-start.3 = (f32[128,4096]{1,0:T(8,128)S(1)}, f32[128,4096]{1,0:T(8,128)}, u32[]{:S(2)}) copy-start(f32[128,4096]{1,0:T(8,128)} %weight_ref.1) | copy-start | bytes 6291460
  20.7 2.1 copy-start.6
  24.5 35.2 %collective-permute-start = (bf16[2,544,1024]{2,1,0:T(8,128)(2,1)}, bf16[2,544,1024]{2,1,0:T(8,128)(2,1)}, u32[]{:S(2)}, u32[]{:S(2)}) collective-permute-start(bf16[2,544,1024]{2,1,0:T(8,128)(2,1)} %broadcast_select_fusion), channel_id=1, source_target_pairs={{0,1},{1,0},{2,3},{3,2},{4,5},{5,4},{6,7},{7,6},{8,9},{9,8},{10,11... | collective-permute-start | bytes 6684680 | tf_op jit(solution)/shard_map/ppermute | solution.py:28
  24.9 4.4 %copy-start.9 = (bf16[128,4096]{1,0:T(8,128)(2,1)S(1)}, bf16[128,4096]{1,0:T(8,128)(2,1)}, u32[]{:S(2)}) copy-start(bf16[128,4096]{1,0:T(8,128)(2,1)} %param.8) | copy-start | bytes 3145732
  24.9 5.5 %copy-start.10 = (bf16[128,256]{1,0:T(8,128)(2,1)S(1)}, bf16[128,256]{1,0:T(8,128)(2,1)}, u32[]{:S(2)}) copy-start(bf16[128,256]{1,0:T(8,128)(2,1)} %param.9) | copy-start | bytes 196612
  30.8 30.3 %slice-start.2 = ((s8[4456448]{0:T(1024)(128)(4,1)}), s8[4194304]{0:T(1024)(128)(4,1)S(1)}, s32[]{:S(2)}) async-start(s8[4456448]{0:T(1024)(128)(4,1)} %bitcast.58), calls=%async_computation.4 | async-start | bytes 8388608
  32.9 28.2 %slice-start.3 = ((s8[4456448]{0:T(1024)(128)(4,1)}), s8[262144]{0:T(1024)(128)(4,1)S(1)}, s32[]{:S(2)}) async-start(s8[4456448]{0:T(1024)(128)(4,1)} %bitcast.58), calls=%async_computation.5 | async-start | bytes 524288
  33.0 23.3 %collective-permute-start.5 = (f32[1,640,256]{2,1,0:T(8,128)S(1)}, f32[1,640,256]{2,1,0:T(8,128)S(1)}, u32[]{:S(2)}, u32[]{:S(2)}) collective-permute-start(f32[1,640,256]{2,1,0:T(8,128)S(1)} %slice_select_fusion.1), channel_id=1, source_target_pairs={{0,2},{1,3},{2,0},{3,1},{4,6},{5,7},{6,4},{7,5},{8,10},{9,11},{10,... | collective-permute-start | bytes 1966088 | tf_op jit(solution)/shard_map/ppermute | solution.py:28
  51.0 64.5 %collective-permute-start.22 = (bf16[128,4096]{1,0:T(8,128)(2,1)}, bf16[128,4096]{1,0:T(8,128)(2,1)S(1)}, u32[]{:S(2)}, u32[]{:S(2)}) collective-permute-start(bf16[128,4096]{1,0:T(8,128)(2,1)} %collective-permute-done.20), channel_id=1, source_target_pairs={{0,4},{4,0},{8,12},{12,8},{16,20},{20,16},{24,28},{28,24},{1,5},{5... | collective-permute-start | bytes 3145736 | tf_op jit(solution)/shard_map/ppermute | solution.py:28
  52.5 41.7 %collective-permute-start.23 = (bf16[128,4096]{1,0:T(8,128)(2,1)}, bf16[128,4096]{1,0:T(8,128)(2,1)S(1)}, u32[]{:S(2)}, u32[]{:S(2)}) collective-permute-start(bf16[128,4096]{1,0:T(8,128)(2,1)} %collective-permute-done.19), channel_id=1, source_target_pairs={{0,8},{4,12},{8,0},{12,4},{16,24},{20,28},{24,16},{28,20},{1,9},{5... | collective-permute-start | bytes 3145736 | tf_op jit(solution)/shard_map/ppermute | solution.py:28
  56.4 33.0 %collective-permute-start.6 = (f32[1,640,256]{2,1,0:T(8,128)S(1)}, f32[1,640,256]{2,1,0:T(8,128)S(1)}, u32[]{:S(2)}, u32[]{:S(2)}) collective-permute-start(f32[1,640,256]{2,1,0:T(8,128)S(1)} %select_select_fusion.3), channel_id=1, source_target_pairs={{0,16},{4,20},{8,24},{12,28},{16,0},{20,4},{24,8},{28,12},{1,17},{... | collective-permute-start | bytes 1966088 | tf_op jit(solution)/shard_map/ppermute | solution.py:28
  59.7 86.2 %collective-permute-start.24 = (bf16[128,4096]{1,0:T(8,128)(2,1)}, bf16[128,4096]{1,0:T(8,128)(2,1)S(1)}, u32[]{:S(2)}, u32[]{:S(2)}) collective-permute-start(bf16[128,4096]{1,0:T(8,128)(2,1)} %collective-permute-done.19), channel_id=1, source_target_pairs={{0,4},{4,0},{8,12},{12,8},{16,20},{20,16},{24,28},{28,24},{1,5},{5... | collective-permute-start | bytes 3145736 | tf_op jit(solution)/shard_map/ppermute | solution.py:28
  89.6 24.2 %collective-permute-start.7 = (f32[1,640,256]{2,1,0:T(8,128)S(1)}, f32[1,640,256]{2,1,0:T(8,128)S(1)}, u32[]{:S(2)}, u32[]{:S(2)}) collective-permute-start(f32[1,640,256]{2,1,0:T(8,128)S(1)} %broadcast_select_fusion.2), channel_id=1, source_target_pairs={{0,4},{4,0},{8,12},{12,8},{16,20},{20,16},{24,28},{28,24},{1,5},{5... | collective-permute-start | bytes 1966088 | tf_op jit(solution)/shard_map/ppermute | solution.py:28
  90.3 26.2 %collective-permute-start.1 = (bf16[1,544,1024]{2,1,0:T(8,128)(2,1)S(1)}, bf16[1,544,1024]{2,1,0:T(8,128)(2,1)S(1)}, u32[]{:S(2)}, u32[]{:S(2)}) collective-permute-start(bf16[1,544,1024]{2,1,0:T(8,128)(2,1)S(1)} %broadcast_select_fusion.1), channel_id=1, source_target_pairs={{0,2},{1,3},{2,0},{3,1},{4,6},{5,7},{6,4},{7,5},{8,10},{9,11},{10,... | collective-permute-start | bytes 3342344 | tf_op jit(solution)/shard_map/ppermute | solution.py:28
  94.2 78.0 %collective-permute-start.25 = (bf16[128,4096]{1,0:T(8,128)(2,1)S(1)}, bf16[128,4096]{1,0:T(8,128)(2,1)S(1)}, u32[]{:S(2)}, u32[]{:S(2)}) collective-permute-start(bf16[128,4096]{1,0:T(8,128)(2,1)S(1)} %collective-permute-done.23), channel_id=1, source_target_pairs={{0,4},{4,0},{8,12},{12,8},{16,20},{20,16},{24,28},{28,24},{1,5},{5... | collective-permute-start | bytes 3145736 | tf_op jit(solution)/shard_map/ppermute | solution.py:28
  113.9 28.8 %collective-permute-start.8 = (f32[1,640,256]{2,1,0:T(8,128)S(1)}, f32[1,640,256]{2,1,0:T(8,128)S(1)}, u32[]{:S(2)}, u32[]{:S(2)}) collective-permute-start(f32[1,640,256]{2,1,0:T(8,128)S(1)} %broadcast_select_fusion.3), channel_id=1, source_target_pairs={{0,8},{4,12},{8,0},{12,4},{16,24},{20,28},{24,16},{28,20},{1,9},{5... | collective-permute-start | bytes 1966088 | tf_op jit(solution)/shard_map/ppermute | solution.py:28
  116.7 30.2 %collective-permute-start.11 = (bf16[512,1024]{1,0:T(8,128)(2,1)S(1)}, bf16[512,1024]{1,0:T(8,128)(2,1)S(1)}, u32[]{:S(2)}, u32[]{:S(2)}) collective-permute-start(bf16[512,1024]{1,0:T(8,128)(2,1)S(1)} %slice_bitcast_fusion), channel_id=1, source_target_pairs={{0,0},{4,4},{2,8},{6,12},{1,16},{5,20},{3,24},{7,28},{8,1},{12,5},... | collective-permute-start | bytes 3145736 | tf_op jit(solution)/shard_map/ppermute | solution.py:63
  142.7 27.5 %collective-permute-start.9 = (f32[1,640,256]{2,1,0:T(8,128)S(1)}, f32[1,640,256]{2,1,0:T(8,128)S(1)}, u32[]{:S(2)}, u32[]{:S(2)}) collective-permute-start(f32[1,640,256]{2,1,0:T(8,128)S(1)} %broadcast_select_fusion.4), channel_id=1, source_target_pairs={{0,2},{1,3},{2,0},{3,1},{4,6},{5,7},{6,4},{7,5},{8,10},{9,11},{10,... | collective-permute-start | bytes 1966088 | tf_op jit(solution)/shard_map/ppermute | solution.py:28
  143.9 39.4 %collective-permute-start.2 = (bf16[1,544,1024]{2,1,0:T(8,128)(2,1)S(1)}, bf16[1,544,1024]{2,1,0:T(8,128)(2,1)S(1)}, u32[]{:S(2)}, u32[]{:S(2)}) collective-permute-start(bf16[1,544,1024]{2,1,0:T(8,128)(2,1)S(1)} %select_select_fusion.2), channel_id=1, source_target_pairs={{0,2},{1,3},{2,0},{3,1},{4,6},{5,7},{6,4},{7,5},{8,10},{9,11},{10,... | collective-permute-start | bytes 3342344 | tf_op jit(solution)/shard_map/ppermute | solution.py:28
  146.9 64.3 %collective-permute-start.12 = (bf16[512,1024]{1,0:T(8,128)(2,1)S(1)}, bf16[512,1024]{1,0:T(8,128)(2,1)}, u32[]{:S(2)}, u32[]{:S(2)}) collective-permute-start(bf16[512,1024]{1,0:T(8,128)(2,1)S(1)} %collective-permute-done.11), channel_id=1, source_target_pairs={{0,16},{4,20},{8,24},{12,28},{16,0},{20,4},{24,8},{28,12},{1,17},{... | collective-permute-start | bytes 3145736 | tf_op jit(solution)/shard_map/ppermute | solution.py:28
  167.7 40.1 %collective-permute-start.13 = (bf16[512,1024]{1,0:T(8,128)(2,1)S(1)}, bf16[512,1024]{1,0:T(8,128)(2,1)}, u32[]{:S(2)}, u32[]{:S(2)}) collective-permute-start(bf16[512,1024]{1,0:T(8,128)(2,1)S(1)} %collective-permute-done.11), channel_id=1, source_target_pairs={{0,8},{4,12},{8,0},{12,4},{16,24},{20,28},{24,16},{28,20},{1,9},{5... | collective-permute-start | bytes 3145736 | tf_op jit(solution)/shard_map/ppermute | solution.py:28
  170.2 44.1 %collective-permute-start.14 = (bf16[512,1024]{1,0:T(8,128)(2,1)S(1)}, bf16[512,1024]{1,0:T(8,128)(2,1)S(1)}, u32[]{:S(2)}, u32[]{:S(2)}) collective-permute-start(bf16[512,1024]{1,0:T(8,128)(2,1)S(1)} %collective-permute-done.11), channel_id=1, source_target_pairs={{0,4},{4,0},{8,12},{12,8},{16,20},{20,16},{24,28},{28,24},{1,5},{5... | collective-permute-start | bytes 3145736 | tf_op jit(solution)/shard_map/ppermute | solution.py:28
  172.2 42.3 %collective-permute-start.10 = (f32[2,640,256]{2,1,0:T(8,128)S(1)}, f32[2,640,256]{2,1,0:T(8,128)S(1)}, u32[]{:S(2)}, u32[]{:S(2)}) collective-permute-start(f32[2,640,256]{2,1,0:T(8,128)S(1)} %maximum_bitcast_fusion.1), channel_id=1, source_target_pairs={{0,1},{1,0},{2,3},{3,2},{4,5},{5,4},{6,7},{7,6},{8,9},{9,8},{10,11... | collective-permute-start | bytes 3932168 | tf_op jit(solution)/shard_map/ppermute | solution.py:28
  183.5 30.8 %copy-start.7 = (bf16[1,1,544,1024]{3,2,1,0:T(8,128)(2,1)}, bf16[1,1,544,1024]{3,2,1,0:T(8,128)(2,1)S(1)}, u32[]{:S(2)}) copy-start(bf16[1,1,544,1024]{3,2,1,0:T(8,128)(2,1)S(1)} %get-tuple-element.25) | copy-start | bytes 3342340
  185.2 128.8 %collective-permute-start.3 = (bf16[2,544,1024]{2,1,0:T(8,128)(2,1)}, bf16[2,544,1024]{2,1,0:T(8,128)(2,1)}, u32[]{:S(2)}, u32[]{:S(2)}) collective-permute-start(bf16[2,544,1024]{2,1,0:T(8,128)(2,1)} %maximum_bitcast_fusion), channel_id=1, source_target_pairs={{0,1},{1,0},{2,3},{3,2},{4,5},{5,4},{6,7},{7,6},{8,9},{9,8},{10,11... | collective-permute-start | bytes 6684680 | tf_op jit(solution)/shard_map/ppermute | solution.py:28
  207.8 99.4 %collective-permute-start.15 = (bf16[512,1024]{1,0:T(8,128)(2,1)}, bf16[512,1024]{1,0:T(8,128)(2,1)}, u32[]{:S(2)}, u32[]{:S(2)}) collective-permute-start(bf16[512,1024]{1,0:T(8,128)(2,1)} %collective-permute-done.13), channel_id=1, source_target_pairs={{0,4},{4,0},{8,12},{12,8},{16,20},{20,16},{24,28},{28,24},{1,5},{5... | collective-permute-start | bytes 3145736 | tf_op jit(solution)/shard_map/ppermute | solution.py:28
  211.2 93.9 %collective-permute-start.16 = (bf16[512,1024]{1,0:T(8,128)(2,1)}, bf16[512,1024]{1,0:T(8,128)(2,1)}, u32[]{:S(2)}, u32[]{:S(2)}) collective-permute-start(bf16[512,1024]{1,0:T(8,128)(2,1)} %collective-permute-done.12), channel_id=1, source_target_pairs={{0,8},{4,12},{8,0},{12,4},{16,24},{20,28},{24,16},{28,20},{1,9},{5... | collective-permute-start | bytes 3145736 | tf_op jit(solution)/shard_map/ppermute | solution.py:28
  214.3 97.4 %collective-permute-start.17 = (bf16[512,1024]{1,0:T(8,128)(2,1)}, bf16[512,1024]{1,0:T(8,128)(2,1)}, u32[]{:S(2)}, u32[]{:S(2)}) collective-permute-start(bf16[512,1024]{1,0:T(8,128)(2,1)} %collective-permute-done.12), channel_id=1, source_target_pairs={{0,4},{4,0},{8,12},{12,8},{16,20},{20,16},{24,28},{28,24},{1,5},{5... | collective-permute-start | bytes 3145736 | tf_op jit(solution)/shard_map/ppermute | solution.py:28
  214.5 4.2 %copy-start = (bf16[4096,1024]{1,0:T(8,128)(2,1)}, bf16[4096,1024]{1,0:T(8,128)(2,1)S(1)}, u32[]{:S(2)}) copy-start(bf16[4096,1024]{1,0:T(8,128)(2,1)S(1)} %constant_dynamic-update-slice_fusion.14) | copy-start | bytes 25165828
  218.7 1.7 copy-start.2
  283.7 2.0 copy-start.4
  285.7 19.4 %all-to-all-start = ((bf16[8,128,128]{2,1,0:T(8,128)(2,1)}), bf16[8,128,128]{2,1,0:T(8,128)(2,1)S(1)}, u32[]{:S(2)}, u32[]{:S(2)}) async-start(bf16[8,128,128]{2,1,0:T(8,128)(2,1)} %get-tuple-element.16), calls=%async_computation | async-start | bytes 524288 | tf_op jit(solution)/shard_map/all_to_all | solution.py:375
  290.1 2.2 copy-start.5
  305.1 8.9 %copy-start.8 = (bf16[1,1,544,1024]{3,2,1,0:T(8,128)(2,1)S(1)}, bf16[1,1,544,1024]{3,2,1,0:T(8,128)(2,1)}, u32[]{:S(2)}) copy-start(bf16[1,1,544,1024]{3,2,1,0:T(8,128)(2,1)} %copy-done.7) | copy-start | bytes 3342340
  305.1 18.9 %collective-permute-start.18 = (bf16[512,1024]{1,0:T(8,128)(2,1)}, bf16[512,1024]{1,0:T(8,128)(2,1)S(1)}, u32[]{:S(2)}, u32[]{:S(2)}) collective-permute-start(bf16[512,1024]{1,0:T(8,128)(2,1)} %collective-permute-done.16), channel_id=1, source_target_pairs={{0,4},{4,0},{8,12},{12,8},{16,20},{20,16},{24,28},{28,24},{1,5},{5... | collective-permute-start | bytes 3145736 | tf_op jit(solution)/shard_map/ppermute | solution.py:28
  316.3 7.7 %slice-start = ((s8[8388608]{0:T(1024)(128)(4,1)}), s8[4194304]{0:T(1024)(128)(4,1)S(1)}, s32[]{:S(2)}) async-start(s8[8388608]{0:T(1024)(128)(4,1)} %bitcast.55), calls=%async_computation.2 | async-start | bytes 8388608
  316.8 7.2 %slice-start.1 = ((s8[8388608]{0:T(1024)(128)(4,1)}), s8[4194304]{0:T(1024)(128)(4,1)S(1)}, s32[]{:S(2)}) async-start(s8[8388608]{0:T(1024)(128)(4,1)} %bitcast.55), calls=%async_computation.3 | async-start | bytes 8388608
  324.1 4.2 %copy-start.1 = (bf16[4096,1024]{1,0:T(8,128)(2,1)}, bf16[4096,1024]{1,0:T(8,128)(2,1)S(1)}, u32[]{:S(2)}) copy-start(bf16[4096,1024]{1,0:T(8,128)(2,1)S(1)} %constant_dynamic-update-slice_fusion.10.panel_ref) | copy-start | bytes 25165828
  334.0 12.8 %collective-permute-start.26 = (f32[1024,128]{1,0:T(8,128)S(1)}, f32[1024,128]{1,0:T(8,128)S(1)}, u32[]{:S(2)}, u32[]{:S(2)}) collective-permute-start(f32[1024,128]{1,0:T(8,128)S(1)} %convolution_subtract_fusion), channel_id=1, source_target_pairs={{0,1},{1,0},{2,3},{3,2},{4,5},{5,4},{6,7},{7,6},{8,9},{9,8},{10,11... | collective-permute-start | bytes 1572872 | tf_op jit(solution)/shard_map/ppermute | solution.py:28
  346.9 32.6 %collective-permute-start.27 = (f32[1024,128]{1,0:T(8,128)S(1)}, f32[1024,128]{1,0:T(8,128)S(1)}, u32[]{:S(2)}, u32[]{:S(2)}) collective-permute-start(f32[1024,128]{1,0:T(8,128)S(1)} %add.233), channel_id=1, source_target_pairs={{0,2},{1,3},{2,0},{3,1},{4,6},{5,7},{6,4},{7,5},{8,10},{9,11},{10,... | collective-permute-start | bytes 1572872 | tf_op jit(solution)/shard_map/ppermute | solution.py:28
  380.4 31.3 %all-to-all-start.1 = ((f32[8,128,128]{2,1,0:T(8,128)}), f32[8,128,128]{2,1,0:T(8,128)S(1)}, u32[]{:S(2)}, u32[]{:S(2)}) async-start(f32[8,128,128]{2,1,0:T(8,128)} %bitcast.25), calls=%async_computation.1 | async-start | bytes 1048576 | tf_op jit(solution)/shard_map/all_to_all | solution.py:401
